TPU v7x, 512 devices: a whole 4x8x8 slice. The times are simulated.
512 devices in a mesh: ta: 32 (over z_hi, x, core), ha: 2 (over z_lo), wa: 8 (over y).
Axes of the slice: x: 4, y: 8, z: 8 (z_hi: 4, z_lo: 2; z = z_hi * 2 + z_lo), core: 2. Of those that a mesh axis runs over, the one named last changes fastest.
Arguments:
- queries: bfloat16 [96, 8, 32, 2048], P('ta', 'ha', 'wa'), may hold values from -6 to 61
- keys: bfloat16 [96, 8, 32, 2048], P('ta', 'ha', 'wa'), may hold values from -6 to 61
- values: bfloat16 [96, 8, 32, 2048], P('ta', 'ha', 'wa'), may hold values from -6 to 6
- query_gain: float32 [128], replicated, may hold values from 0.5 to 5
- key_gain: float32 [128], replicated, may hold values from 0.5 to 5
Outputs:
- attended: bfloat16 [96, 8, 32, 2048], P('ta', 'ha', 'wa')
All inputs are finite; a program needn't handle non-finite values.
Results may differ from a plain program's by a relative error of at most 0.0025.
The roundings to bfloat16 on the way count: a program that leaves them out, or rounds other values in their place, can miss the bound.
Values may be sent and summed in bfloat16 or wider, within the bound.
A program may use at most 64 MiB of HBM per device.

v0:
```python
import math

import jax
import jax.numpy as jnp
from jax import lax
from jax.sharding import PartitionSpec as P

TILE_T = 6
TILE_H = 8
TILE_W = 8


epsilon = 1e-06


def extended_2(block, sides, width):
    for axis, dim in sides:
        count = lax.axis_size(axis)
        forward = [(i, i + 1) for i in range(count - 1)]
        backward = [(target, source) for source, target in forward]
        low = lax.ppermute(
            lax.slice_in_dim(block, block.shape[dim] - width, None, axis=dim), axis, forward
        )
        high = lax.ppermute(lax.slice_in_dim(block, 0, width, axis=dim), axis, backward)
        block = jnp.concatenate([low, block, high], axis=dim)
    return block


def normalize(tensor, gain_vec):
    head_dim = gain_vec.shape[0]
    per_head = tensor.astype(jnp.float32).reshape(
        tensor.shape[:-1] + (tensor.shape[-1] // head_dim, head_dim)
    )
    mean_sq = jnp.mean(per_head * per_head, axis=-1, keepdims=True)
    scaled = per_head * lax.rsqrt(mean_sq + epsilon) * gain_vec
    return scaled.reshape(tensor.shape).astype(jnp.bfloat16)


def block_count(item_count, query_len):
    for divisor in range(1, item_count + 1):
        if item_count % divisor == 0 and divisor * query_len >= 384:
            return divisor
    return item_count


def frame_window(keys_values):
    frames = keys_values.shape[0]
    lower_parts = []
    upper_parts = []
    current = keys_values
    for round_index in range(3):
        padded = extended_2(current, (("ta", 0),), frames)
        lower = padded[:frames]
        upper = padded[padded.shape[0] - frames :]
        lower_parts.insert(0, lower)
        upper_parts.append(upper)
        current = jnp.concatenate((upper, lower), axis=0)
    extended = jnp.concatenate(lower_parts + [keys_values] + upper_parts, axis=0)
    return extended


def attend(q_head, kv_ext, frame_start, tile_frame, tile_grand_count, row_offset):
    frames, q_high, wide, head_dim = q_head.shape
    key_rows = kv_ext.shape[1]
    q_tile_h = min(TILE_H, q_high)
    q_row_blocks = q_high // q_tile_h
    row_tiles = key_rows // TILE_H
    col_tiles = wide // TILE_W
    row_window_span = min(3, row_tiles)
    col_win = min(3, col_tiles)
    query_len = frames * q_tile_h * TILE_W
    item_count = q_row_blocks * col_tiles
    per_step = block_count(item_count, query_len)
    score_scale = 1.0 / math.sqrt(head_dim)
    frame_index = tile_frame - 1 + jnp.arange(3, dtype=jnp.int32)
    frame_good = (frame_index >= 0) & (frame_index < tile_grand_count)
    zero_index = jnp.zeros((), jnp.int32)

    def window(item):
        local_block = item // col_tiles
        tile_col = item % col_tiles
        tile_row = (row_offset + local_block * q_tile_h) // TILE_H
        q_anchor = (zero_index, local_block * q_tile_h, tile_col * TILE_W, zero_index)
        query_tile = lax.dynamic_slice(
            q_head, q_anchor, (frames, q_tile_h, TILE_W, head_dim)
        ).reshape(query_len, head_dim)
        row_first = jnp.clip(tile_row - 1, 0, row_tiles - row_window_span)
        col_first = jnp.clip(tile_col - 1, 0, col_tiles - col_win)
        k_anchor = (frame_start, row_first * TILE_H, col_first * TILE_W, zero_index, zero_index)
        nearby = lax.dynamic_slice(
            kv_ext, k_anchor, (3 * TILE_T, row_window_span * TILE_H, col_win * TILE_W, 2, head_dim)
        )
        key_tile = nearby[:, :, :, 0, :].reshape(-1, head_dim)
        value_tile = nearby[:, :, :, 1, :].reshape(-1, head_dim)
        row_good = jnp.abs(row_first + jnp.arange(row_window_span, dtype=jnp.int32) - tile_row) <= 1
        col_good = jnp.abs(col_first + jnp.arange(col_win, dtype=jnp.int32) - tile_col) <= 1
        key_ok = (
            frame_good[:, None, None, None, None, None]
            & row_good[None, None, :, None, None, None]
            & col_good[None, None, None, None, :, None]
        )
        key_ok = jnp.broadcast_to(
            key_ok, (3, TILE_T, row_window_span, TILE_H, col_win, TILE_W)
        ).reshape(-1)
        return (query_tile, key_tile, value_tile, key_ok)

    def run_step(iteration_index):
        item_ids = iteration_index * per_step + jnp.arange(per_step, dtype=jnp.int32)
        query_block_rows, key_block_rows, value_block, key_ok = jax.vmap(window)(item_ids)
        scores = (
            jnp.einsum(
                "yeo,yxo->yex", query_block_rows, key_block_rows, preferred_element_type=jnp.float32
            )
            * score_scale
        )
        scores = jnp.where(key_ok[:, None, :], scores, -jnp.inf)
        row_max = jnp.max(scores, axis=2, keepdims=True)
        weights = jnp.exp(scores - row_max)
        row_total = jnp.sum(weights, axis=2, keepdims=True)
        summed = jnp.einsum(
            "fgo,fou->fgu",
            weights.astype(jnp.bfloat16),
            value_block,
            preferred_element_type=jnp.float32,
        )
        return (summed / row_total).astype(jnp.bfloat16)

    outputs = lax.map(run_step, jnp.arange(item_count // per_step, dtype=jnp.int32))
    outputs = outputs.reshape(q_row_blocks, col_tiles, frames, q_tile_h, TILE_W, head_dim)
    return outputs.transpose(2, 0, 3, 1, 4, 5).reshape(frames, q_high, wide, head_dim)


def all_heads(
    part_q, part_k, part_v, head_dim, frame_start, tile_frame, tile_grand_count, row_offset
):
    keys_values = jnp.stack((part_k, part_v), axis=3)
    extended = frame_window(keys_values)
    outputs = []
    for group in range(part_q.shape[3] // head_dim):
        low = group * head_dim
        outputs.append(
            attend(
                part_q[..., low : low + head_dim],
                extended[..., low : low + head_dim],
                frame_start,
                tile_frame,
                tile_grand_count,
                row_offset,
            )
        )
    return jnp.concatenate(outputs, axis=3)


def per_device(queries, keys, values, query_gain, key_gain):
    frames, row_count, col_count, feature_width = queries.shape
    head_dim = query_gain.shape[0]
    normed_q = normalize(queries, query_gain)
    normed_k = normalize(keys, key_gain)
    frame_first = lax.axis_index("ta") * frames
    tile_frame = frame_first // TILE_T
    frame_start = 3 * frames - TILE_T - frame_first % TILE_T
    tile_grand_count = lax.axis_size("ta") * frames // TILE_T
    part_q, part_k, part_v = (
        lax.all_to_all(normed_q, "wa", split_axis=3, concat_axis=2, tiled=True),
        lax.all_to_all(normed_k, "wa", split_axis=3, concat_axis=2, tiled=True),
        lax.all_to_all(values, "wa", split_axis=3, concat_axis=2, tiled=True),
    )
    part_k, part_v = (
        lax.all_gather(part_k, "ha", axis=1, tiled=True),
        lax.all_gather(part_v, "ha", axis=1, tiled=True),
    )
    row_offset = lax.axis_index("ha") * row_count
    attended = all_heads(
        part_q, part_k, part_v, head_dim, frame_start, tile_frame, tile_grand_count, row_offset
    )
    result = lax.all_to_all(attended, "wa", split_axis=2, concat_axis=3, tiled=True)
    return result


def solution(mesh):
    return jax.shard_map(
        per_device,
        mesh=mesh,
        in_specs=(
            P("ta", "ha", "wa", None),
            P("ta", "ha", "wa", None),
            P("ta", "ha", "wa", None),
            P(),
            P(),
        ),
        out_specs=P("ta", "ha", "wa", None),
        check_vma=False,
    )
```

profile of v0, /device:TPU:71, one launch (start us, length us, event | category | flops | bytes accessed | tf_op | source)
XLA Modules:
  0.0 297.3 jit_solution(15681837758204378570)
XLA Ops:
  0.0 1.0 convert_multiply_fusion.1
  1.7 1.1 fusion.27
  2.8 7.2 %copy.60 = bf16[3,4,4,2048]{2,1,0,3:T(4,128)(2,1)} copy(bf16[3,4,4,2048]{3,2,1,0:T(4,128)(2,1)S(1)} %fusion.27) | data formatting | bytes 393216 | tf_op jit(solution)/shard_map/convert_element_type | solution.py:36
  10.0 13.9 %reshape.382 = bf16[8,2,6144]{2,1,0:T(2,128)(2,1)} reshape(bf16[2048,3,4,4]{3,2,1,0:T(4,128)(2,1)} %bitcast.73) | data formatting | bytes 393216
  23.9 6.8 %all-to-all-start.1 = ((bf16[8,2,6144]{2,1,0:T(2,128)(2,1)}), bf16[8,2,6144]{2,1,0:T(2,128)(2,1)S(1)}, u32[]{:S(2)}, u32[]{:S(2)}) async-start(bf16[8,2,6144]{2,1,0:T(2,128)(2,1)} %reshape.382), calls=%async_computation.1 | async-start | bytes 393216 | tf_op jit(solution)/shard_map/all_to_all | solution.py:165
  30.7 7.2 %copy.63 = bf16[3,4,4,2048]{2,1,0,3:T(4,128)(2,1)} copy(bf16[3,4,4,2048]{3,2,1,0:T(4,128)(2,1)S(1)} %copy-done.3) | data formatting | bytes 393216 | tf_op args[2]
  37.9 13.9 %reshape.380 = bf16[8,2,6144]{2,1,0:T(2,128)(2,1)} reshape(bf16[2048,3,4,4]{3,2,1,0:T(4,128)(2,1)} %bitcast.78) | data formatting | bytes 393216
  51.8 6.6 %all-to-all-start.2 = ((bf16[8,2,6144]{2,1,0:T(2,128)(2,1)}), bf16[8,2,6144]{2,1,0:T(2,128)(2,1)S(1)}, u32[]{:S(2)}, u32[]{:S(2)}) async-start(bf16[8,2,6144]{2,1,0:T(2,128)(2,1)} %reshape.380), calls=%async_computation.2 | async-start | bytes 393216 | tf_op jit(solution)/shard_map/all_to_all | solution.py:166
  58.4 14.7 %reshape.383 = bf16[2048,3,4,4]{3,2,1,0:T(4,128)(2,1)} reshape(bf16[8,2,6144]{2,1,0:T(2,128)(2,1)S(1)} %all-to-all-done.1) | data formatting | bytes 393216
  73.1 9.1 %copy.61 = bf16[3,4,8,4,256]{4,3,2,0,1:T(4,128)(2,1)S(1)} copy(bf16[3,4,8,4,256]{3,1,0,4,2:T(4,128)(2,1)} %bitcast.74) | data formatting | bytes 393216 | tf_op jit(solution)/shard_map/all_to_all | solution.py:165
  82.3 5.7 %all_gather.6 = bf16[3,8,32,256]{3,2,0,1:T(8,128)(2,1)S(1)} all-gather(bf16[3,4,32,256]{3,2,0,1:T(8,128)(2,1)S(1)} %all_to_all.59), channel_id=1, replica_groups=mesh['ta'=32,'ha'=2,'wa'=8] {'ha'}, dimensions={1}, use_global_device_ids=true | all-gather | bytes 589824 | tf_op jit(solution)/shard_map/all_gather | solution.py:169
  88.3 14.7 %reshape.381 = bf16[2048,3,4,4]{3,2,1,0:T(4,128)(2,1)} reshape(bf16[8,2,6144]{2,1,0:T(2,128)(2,1)S(1)} %all-to-all-done.2) | data formatting | bytes 393216
  102.9 9.2 %copy.64 = bf16[3,4,8,4,256]{4,3,2,0,1:T(4,128)(2,1)S(1)} copy(bf16[3,4,8,4,256]{3,1,0,4,2:T(4,128)(2,1)} %bitcast.75) | data formatting | bytes 393216 | tf_op jit(solution)/shard_map/all_to_all | solution.py:166
  112.2 5.2 %all_gather.7 = bf16[3,8,32,256]{3,2,0,1:T(8,128)(2,1)S(1)} all-gather(bf16[3,4,32,256]{3,2,0,1:T(8,128)(2,1)S(1)} %all_to_all.63), channel_id=1, replica_groups=mesh['ta'=32,'ha'=2,'wa'=8] {'ha'}, dimensions={1}, use_global_device_ids=true | all-gather | bytes 589824 | tf_op jit(solution)/shard_map/all_gather | solution.py:170
  117.6 1.0 pad_maximum_fusion
  118.6 9.2 %collective-permute-start = (bf16[3,8,32,2,256]{4,1,3,2,0:T(8,128)(2,1)}, bf16[3,8,32,2,256]{4,1,3,2,0:T(8,128)(2,1)S(1)}, u32[]{:S(2)}, u32[]{:S(2)}) collective-permute-start(bf16[3,8,32,2,256]{4,1,3,2,0:T(8,128)(2,1)} %pad_maximum_fusion), channel_id=1, source_target_pairs={{0,16},{16,32},{32,48},{48,64},{64,80},{80,96},{96,112},{112,128},... | collective-permute-start | bytes 2359304 | tf_op jit(solution)/shard_map/ppermute | solution.py:21
  128.6 1.9 collective-permute-start.3
  130.5 23.1 %collective-permute-done = bf16[3,8,32,2,256]{4,1,3,2,0:T(8,128)(2,1)S(1)} collective-permute-done((bf16[3,8,32,2,256]{4,1,3,2,0:T(8,128)(2,1)}, bf16[3,8,32,2,256]{4,1,3,2,0:T(8,128)(2,1)S(1)}, u32[]{:S(2)}, u32[]{:S(2)}) %collective-permute-start) | collective-permute-done | bytes 786464 | tf_op jit(solution)/shard_map/ppermute | solution.py:21
  153.6 7.2 %collective-permute-start.1 = (bf16[3,8,32,2,256]{4,1,3,2,0:T(8,128)(2,1)S(1)}, bf16[3,8,32,2,256]{4,1,3,2,0:T(8,128)(2,1)}, u32[]{:S(2)}, u32[]{:S(2)}) collective-permute-start(bf16[3,8,32,2,256]{4,1,3,2,0:T(8,128)(2,1)S(1)} %collective-permute-done), channel_id=1, source_target_pairs={{0,16},{16,32},{32,48},{48,64},{64,80},{80,96},{96,112},{112,128},... | collective-permute-start | bytes 2359304 | tf_op jit(solution)/shard_map/ppermute | solution.py:21
  161.0 7.2 %copy.57 = bf16[3,4,4,2048]{2,1,0,3:T(4,128)(2,1)} copy(bf16[3,4,4,2048]{3,2,1,0:T(4,128)(2,1)S(1)} %fusion.25) | data formatting | bytes 393216 | tf_op jit(solution)/shard_map/convert_element_type | solution.py:36
  168.2 13.9 %reshape.384 = bf16[8,2,6144]{2,1,0:T(2,128)(2,1)} reshape(bf16[2048,3,4,4]{3,2,1,0:T(4,128)(2,1)} %bitcast.76) | data formatting | bytes 393216
  182.1 6.6 %all-to-all-start = ((bf16[8,2,6144]{2,1,0:T(2,128)(2,1)}), bf16[8,2,6144]{2,1,0:T(2,128)(2,1)S(1)}, u32[]{:S(2)}, u32[]{:S(2)}) async-start(bf16[8,2,6144]{2,1,0:T(2,128)(2,1)} %reshape.384), calls=%async_computation | async-start | bytes 393216 | tf_op jit(solution)/shard_map/all_to_all | solution.py:164
  188.8 1.9 collective-permute-start.4
  190.8 6.7 %collective-permute-start.2 = (bf16[3,8,32,2,256]{4,1,3,2,0:T(8,128)(2,1)}, bf16[3,8,32,2,256]{4,1,3,2,0:T(8,128)(2,1)}, u32[]{:S(2)}, u32[]{:S(2)}) collective-permute-start(bf16[3,8,32,2,256]{4,1,3,2,0:T(8,128)(2,1)} %collective-permute-done.1), channel_id=1, source_target_pairs={{0,16},{16,32},{32,48},{48,64},{64,80},{80,96},{96,112},{112,128},... | collective-permute-start | bytes 2359304 | tf_op jit(solution)/shard_map/ppermute | solution.py:21
  198.5 14.7 %reshape.385 = bf16[2048,3,4,4]{3,2,1,0:T(4,128)(2,1)} reshape(bf16[8,2,6144]{2,1,0:T(2,128)(2,1)S(1)} %all-to-all-done) | data formatting | bytes 393216
  213.1 9.1 %copy.58 = bf16[3,4,4,8,256]{4,1,0,2,3:T(4,128)(2,1)S(1)} copy(bf16[3,4,4,8,256]{2,1,0,4,3:T(4,128)(2,1)} %bitcast.77) | data formatting | bytes 393216 | tf_op jit(solution)/shard_map/all_to_all | solution.py:164
  223.6 2.1 collective-permute-start.5
  225.8 1.2 constant_dynamic-update-slice_fusion.6
  227.0 1.2 constant_dynamic-update-slice_fusion.5
  228.4 1.2 constant_dynamic-update-slice_fusion.1
  229.6 17.6 %collective-permute-done.5 = bf16[3,8,32,2,256]{4,1,3,2,0:T(8,128)(2,1)S(1)} collective-permute-done((bf16[3,8,32,2,256]{4,1,3,2,0:T(8,128)(2,1)}, bf16[3,8,32,2,256]{4,1,3,2,0:T(8,128)(2,1)S(1)}, u32[]{:S(2)}, u32[]{:S(2)}) %collective-permute-start.5) | collective-permute-done | bytes 786464 | tf_op jit(solution)/shard_map/ppermute | solution.py:24
  247.3 3.1 %fusion.46 = (bf16[21,8,32,2,128]{4,1,3,2,0:T(8,128)(2,1)}, bf16[21,8,32,2,128]{4,1,3,2,0:T(8,128)(2,1)S(1)}) fusion(bf16[21,8,32,2,256]{4,1,3,2,0:T(8,128)(2,1)S(1)} %constant_dynamic-update-slice_fusion), kind=kLoop, calls=%fused_computation.93 | loop fusion | bytes 11010048 | tf_op jit(solution)/shard_map/slice | solution.py:144
  250.4 6.2 %gather_fusion.1 = bf16[4,18,8,24,2,128]{5,2,4,3,1,0:T(8,128)(2,1)} fusion(bf16[21,8,32,2,128]{4,1,3,2,0:T(8,128)(2,1)} %get-tuple-element.42, s32[4]{0:T(128)S(1)} %fusion.42), kind=kCustom, calls=%fused_computation.1 | custom fusion | bytes 14155856 | tf_op jit(solution)/shard_map/while/body/eval_jaxpr/vmap()/gather | solution.py:90
  256.5 4.5 %fusion.44 = (bf16[4,18,8,24,1,128]{5,2,4,3,1,0:T(8,128)(2,1)S(1)}, bf16[4,18,8,24,1,128]{5,2,4,3,1,0:T(8,128)(2,1)S(1)}) fusion(bf16[4,18,8,24,2,128]{5,2,4,3,1,0:T(8,128)(2,1)} %gather_fusion.1), kind=kLoop, calls=%fused_computation.91 | loop fusion | bytes 14155776 | tf_op jit(solution)/shard_map/while/body/eval_jaxpr/vmap()/slice | solution.py:93
  261.0 1.1 copy.66
  262.1 1.1 copy.67
  263.2 1.4 fusion.49
  264.6 0.9 fusion.2
  265.4 1.0 fusion.15
  266.5 4.4 %gather_fusion.3 = bf16[4,18,8,24,2,128]{5,2,4,3,1,0:T(8,128)(2,1)} fusion(bf16[21,8,32,2,128]{4,1,3,2,0:T(8,128)(2,1)S(1)} %get-tuple-element.43, s32[4]{0:T(128)S(1)} %fusion.42), kind=kCustom, calls=%fused_computation.3 | custom fusion | bytes 14155856 | tf_op jit(solution)/shard_map/while/body/eval_jaxpr/vmap()/gather | solution.py:90
  270.9 4.5 %fusion.45 = (bf16[4,18,8,24,1,128]{5,2,4,3,1,0:T(8,128)(2,1)S(1)}, bf16[4,18,8,24,1,128]{5,2,4,3,1,0:T(8,128)(2,1)S(1)}) fusion(bf16[4,18,8,24,2,128]{5,2,4,3,1,0:T(8,128)(2,1)} %gather_fusion.3), kind=kLoop, calls=%fused_computation.92 | loop fusion | bytes 14155776 | tf_op jit(solution)/shard_map/while/body/eval_jaxpr/vmap()/slice | solution.py:93
  275.4 1.1 copy.70
  276.5 1.1 copy.71
  277.5 1.6 fusion.48
  279.2 0.9 fusion.4
  280.1 1.0 fusion.21
  281.3 15.1 %all_to_all.72 = bf16[3,4,32,256]{3,1,0,2:T(4,128)(2,1)S(1)} all-to-all(bf16[3,4,32,256]{3,1,0,2:T(4,128)(2,1)S(1)} %copy.73), channel_id=1, replica_groups=mesh['ta'=32,'ha'=2,'wa'=8] {'wa'}, dimensions={2} | all-to-all | bytes 393216 | tf_op jit(solution)/shard_map/all_to_all | solution.py:176
  296.5 0.8 all_to_all.67
  (59 shorter events, 5.2 us)
Async XLA Ops:
  0.0 1.7 copy-start
  2.8 27.9 %copy-start.3 = (bf16[3,4,4,2048]{3,2,1,0:T(4,128)(2,1)S(1)}, bf16[3,4,4,2048]{3,2,1,0:T(4,128)(2,1)}, u32[]{:S(2)}) copy-start(bf16[3,4,4,2048]{3,2,1,0:T(4,128)(2,1)} %param.7) | copy-start | bytes 589828
  23.9 27.9 %all-to-all-start.1 = ((bf16[8,2,6144]{2,1,0:T(2,128)(2,1)}), bf16[8,2,6144]{2,1,0:T(2,128)(2,1)S(1)}, u32[]{:S(2)}, u32[]{:S(2)}) async-start(bf16[8,2,6144]{2,1,0:T(2,128)(2,1)} %reshape.382), calls=%async_computation.1 | async-start | bytes 393216 | tf_op jit(solution)/shard_map/all_to_all | solution.py:165
  51.8 36.5 %all-to-all-start.2 = ((bf16[8,2,6144]{2,1,0:T(2,128)(2,1)}), bf16[8,2,6144]{2,1,0:T(2,128)(2,1)S(1)}, u32[]{:S(2)}, u32[]{:S(2)}) async-start(bf16[8,2,6144]{2,1,0:T(2,128)(2,1)} %reshape.380), calls=%async_computation.2 | async-start | bytes 393216 | tf_op jit(solution)/shard_map/all_to_all | solution.py:166
  102.9 24.8 %copy-start.2 = (bf16[3,4,4,2048]{3,2,1,0:T(4,128)(2,1)S(1)}, bf16[3,4,4,2048]{3,2,1,0:T(4,128)(2,1)}, u32[]{:S(2)}) copy-start(bf16[3,4,4,2048]{3,2,1,0:T(4,128)(2,1)} %param.5) | copy-start | bytes 589828
  102.9 25.6 %copy-start.4 = (f32[128]{0:T(128)S(1)}, f32[128]{0:T(128)}, u32[]{:S(2)}) copy-start(f32[128]{0:T(128)} %param.8) | copy-start | bytes 1540
  118.6 35.1 %collective-permute-start = (bf16[3,8,32,2,256]{4,1,3,2,0:T(8,128)(2,1)}, bf16[3,8,32,2,256]{4,1,3,2,0:T(8,128)(2,1)S(1)}, u32[]{:S(2)}, u32[]{:S(2)}) collective-permute-start(bf16[3,8,32,2,256]{4,1,3,2,0:T(8,128)(2,1)} %pad_maximum_fusion), channel_id=1, source_target_pairs={{0,16},{16,32},{32,48},{48,64},{64,80},{80,96},{96,112},{112,128},... | collective-permute-start | bytes 2359304 | tf_op jit(solution)/shard_map/ppermute | solution.py:21
  128.6 60.3 %collective-permute-start.3 = (bf16[3,8,32,2,256]{4,1,3,2,0:T(8,128)(2,1)}, bf16[3,8,32,2,256]{4,1,3,2,0:T(8,128)(2,1)S(1)}, u32[]{:S(2)}, u32[]{:S(2)}) collective-permute-start(bf16[3,8,32,2,256]{4,1,3,2,0:T(8,128)(2,1)} %pad_maximum_fusion), channel_id=1, source_target_pairs={{16,0},{32,16},{48,32},{64,48},{80,64},{96,80},{112,96},{128,112},... | collective-permute-start | bytes 2359304 | tf_op jit(solution)/shard_map/ppermute | solution.py:24
  153.6 37.1 %collective-permute-start.1 = (bf16[3,8,32,2,256]{4,1,3,2,0:T(8,128)(2,1)S(1)}, bf16[3,8,32,2,256]{4,1,3,2,0:T(8,128)(2,1)}, u32[]{:S(2)}, u32[]{:S(2)}) collective-permute-start(bf16[3,8,32,2,256]{4,1,3,2,0:T(8,128)(2,1)S(1)} %collective-permute-done), channel_id=1, source_target_pairs={{0,16},{16,32},{32,48},{48,64},{64,80},{80,96},{96,112},{112,128},... | collective-permute-start | bytes 2359304 | tf_op jit(solution)/shard_map/ppermute | solution.py:21
  182.1 16.4 %all-to-all-start = ((bf16[8,2,6144]{2,1,0:T(2,128)(2,1)}), bf16[8,2,6144]{2,1,0:T(2,128)(2,1)S(1)}, u32[]{:S(2)}, u32[]{:S(2)}) async-start(bf16[8,2,6144]{2,1,0:T(2,128)(2,1)} %reshape.384), calls=%async_computation | async-start | bytes 393216 | tf_op jit(solution)/shard_map/all_to_all | solution.py:164
  188.8 34.8 %collective-permute-start.4 = (bf16[3,8,32,2,256]{4,1,3,2,0:T(8,128)(2,1)S(1)}, bf16[3,8,32,2,256]{4,1,3,2,0:T(8,128)(2,1)}, u32[]{:S(2)}, u32[]{:S(2)}) collective-permute-start(bf16[3,8,32,2,256]{4,1,3,2,0:T(8,128)(2,1)S(1)} %collective-permute-done.3), channel_id=1, source_target_pairs={{16,0},{32,16},{48,32},{64,48},{80,64},{96,80},{112,96},{128,112},... | collective-permute-start | bytes 2359304 | tf_op jit(solution)/shard_map/ppermute | solution.py:24
  190.8 35.0 %collective-permute-start.2 = (bf16[3,8,32,2,256]{4,1,3,2,0:T(8,128)(2,1)}, bf16[3,8,32,2,256]{4,1,3,2,0:T(8,128)(2,1)}, u32[]{:S(2)}, u32[]{:S(2)}) collective-permute-start(bf16[3,8,32,2,256]{4,1,3,2,0:T(8,128)(2,1)} %collective-permute-done.1), channel_id=1, source_target_pairs={{0,16},{16,32},{32,48},{48,64},{64,80},{80,96},{96,112},{112,128},... | collective-permute-start | bytes 2359304 | tf_op jit(solution)/shard_map/ppermute | solution.py:21
  223.6 23.6 %collective-permute-start.5 = (bf16[3,8,32,2,256]{4,1,3,2,0:T(8,128)(2,1)}, bf16[3,8,32,2,256]{4,1,3,2,0:T(8,128)(2,1)S(1)}, u32[]{:S(2)}, u32[]{:S(2)}) collective-permute-start(bf16[3,8,32,2,256]{4,1,3,2,0:T(8,128)(2,1)} %collective-permute-done.4), channel_id=1, source_target_pairs={{16,0},{32,16},{48,32},{64,48},{80,64},{96,80},{112,96},{128,112},... | collective-permute-start | bytes 2359304 | tf_op jit(solution)/shard_map/ppermute | solution.py:24
  280.1 17.2 %copy-start.1 = (f32[128]{0:T(128)S(1)}, f32[128]{0:T(128)}, u32[]{:S(2)}) copy-start(f32[128]{0:T(128)} %param.9) | copy-start | bytes 1540
where the time goes:
time: 299 us; the launch traced here: 297 us
  local copies, waits for them, and re-layouts  170 us (57%)
  starting transfers between devices  49.1 us (16%)
  waiting for transfers between devices  40.8 us (14%)
  blocking collectives  26 us (9%)
  other arithmetic  5.68 us (2%)
  matrix products  5.1 us (2%)
    unnamed x22, local copies, waits for them, and re-layouts  96.5 us
    ppermute x3, waiting for transfers between devices, extended_2(): lax.ppermute(lax.slice_in_dim(block, block.shape[dim] - width, None, axis...  23.1 us
    ppermute x3, starting transfers between devices, extended_2(): lax.ppermute(lax.slice_in_dim(block, block.shape[dim] - width, None, axis...  23.1 us
    ppermute x3, waiting for transfers between devices, extended_2(): lax.ppermute(lax.slice_in_dim(block, 0, width, axis=dim), axis, backward)  17.6 us
    all_to_all x1, blocking collectives, per_device(): lax.all_to_all(attended, 'wa', split_axis=2, concat_axis=3, tiled=True)  15.1 us
    convert_element_type x2, local copies, waits for them, and re-layouts, normalize(): return scaled.reshape(tensor.shape).astype(jnp.bfloat16)  14.4 us
    slice x4, local copies, waits for them, and re-layouts, window(): key_tile = nearby[:, :, :, 0, :].reshape(-1, head_dim)  11.1 us
    gather x2, local copies, waits for them, and re-layouts, window(): lax.dynamic_slice(kv_ext, k_anchor, (3 * TILE_T, row_window_span * TILE_H...  10.5 us
  transfers between devices with their start and end apart: 9, of which 2 were waited for; matrix products, arithmetic and copies ran while one was open for 33% of the time, Pallas kernels for 0%

commit v1 on v0

v1 whole, which is shorter than its diff:
```python
import functools
import math

import jax
import jax.numpy as jnp
from jax import lax
from jax.experimental import pallas as pl
from jax.experimental.pallas import tpu as pltpu
from jax.sharding import PartitionSpec as P

MESH = pl.DeviceIdType.MESH
EPSILON = 1e-06
HEADS = 16
DIM = 128
TOKENS = 48
SOURCES = 8
TILE = SOURCES * TOKENS
HALF = TILE // 2
SCORE_SCALE = 1.0 / math.sqrt(DIM)
EXP2_SCALE = SCORE_SCALE * math.log2(math.e)


def normed(x, gain):
    mean_sq = jnp.mean(x * x, axis=-1, keepdims=True)
    return x * lax.rsqrt(mean_sq + EPSILON) * gain


def kernel(
    q_ref, k_ref, v_ref, qg_ref, kg_ref, o_ref,
    qs, ks, vs, qb, kb, vb, osend, ob, s_narrow, s_wide, m_ref, l_ref, acc_ref,
    own_send, own_self, q_recv, k_recv, v_recv, k_edge, v_edge, k_near, v_near,
    fwd_send, out_send, out_recv,
):
    ta, zl, y = lax.axis_index("ta"), lax.axis_index("ha"), lax.axis_index("wa")
    frame, core = ta // 2, lax.rem(ta, 2)
    last_frame = lax.axis_size("ta") // 2 - 1
    chip = y * 2 + zl
    to_core = y // 4
    own = core == to_core
    has_low, has_high = frame > 0, frame < last_frame

    def device(f, c, z, w):
        return {"ta": f * 2 + c, "ha": z, "wa": w}

    barrier = pltpu.get_barrier_semaphore()

    def greet(f, c, z, w):
        pl.semaphore_signal(barrier, inc=1, device_id=device(f, c, z, w), device_id_type=MESH)

    def greet_step(n, carry):
        @pl.when(jnp.logical_or(n != chip, jnp.logical_not(own)))
        def _():
            greet(frame, to_core, lax.rem(n, 2), n // 2)

        z, c, w = lax.rem(n // 2, 2), lax.rem(n, 2), core * 4 + n // 4
        @pl.when(jnp.logical_or(z * 1 + w * 2 != chip, c != core))
        def _():
            greet(frame, c, z, w)

        return carry

    lax.fori_loop(0, HEADS, greet_step, 0)
    greet(frame, 1 - core, zl, y)

    @pl.when(has_low)
    def _():
        greet(frame - 1, 0, zl, y)
        greet(frame - 1, 1, zl, y)

    @pl.when(has_high)
    def _():
        greet(frame + 1, 0, zl, y)
        greet(frame + 1, 1, zl, y)

    for n in range(HEADS):
        lanes = slice(n * DIM, (n + 1) * DIM)
        k = k_ref[:, :, :, lanes].astype(jnp.float32).reshape(TOKENS, DIM)
        ks[n] = normed(k, kg_ref[...]).astype(jnp.bfloat16)
    for n in range(HEADS):
        lanes = slice(n * DIM, (n + 1) * DIM)
        q = q_ref[:, :, :, lanes].astype(jnp.float32).reshape(TOKENS, DIM)
        qs[n] = normed(q, qg_ref[...]).astype(jnp.bfloat16)
        v = v_ref[:, :, :, lanes].astype(jnp.float32).reshape(TOKENS, DIM)
        vs[n] = v.astype(jnp.bfloat16)

    greetings = (
        1 + 2 * HEADS
        - jnp.where(own, 2, 0)
        + jnp.where(has_low, 2, 0)
        + jnp.where(has_high, 2, 0)
    )
    pl.semaphore_wait(barrier, greetings)

    col = y // 2
    tile = lax.rem(col, 2)
    rows = pl.ds((lax.rem(y, 2) * 4 + zl * 2 + core) * TOKENS, TOKENS)
    k_to = kb.at[1, col - to_core, rows]
    v_to = vb.at[1, col - to_core, rows]
    q_to = qb.at[tile, rows]
    group = tile * 2 + lax.rem(y, 2)

    def block_send(which, source, target, recv, n):
        return pltpu.make_async_remote_copy(
            src_ref=source.at[n], dst_ref=target,
            send_sem=own_send.at[which], recv_sem=recv,
            device_id=device(frame, to_core, lax.rem(n, 2), n // 2), device_id_type=MESH,
        )

    blocks = (
        (0, ks, k_to, k_recv.at[group]),
        (1, qs, q_to, q_recv.at[tile]),
        (2, vs, v_to, v_recv.at[group]),
    )

    def block_self(which, source, target, recv):
        return (
            pltpu.make_async_copy(source.at[chip], target, recv),
            pltpu.make_async_remote_copy(
                src_ref=source.at[chip], dst_ref=target,
                send_sem=own_self.at[which], recv_sem=recv,
                device_id=device(frame, 1 - core, zl, y), device_id_type=MESH,
            ),
        )

    for which, source, target, recv in blocks:
        here, there = block_self(which, source, target, recv)

        @pl.when(own)
        def _(here=here):
            here.start()

        @pl.when(jnp.logical_not(own))
        def _(there=there):
            there.start()

        def send_step(j, carry, which=which, source=source, target=target, recv=recv):
            turn = j // 2
            offset = (turn + 1) // 2 * (2 * lax.rem(turn, 2) - 1)
            to_y = lax.rem(y + offset + 8, 8)
            to_z = lax.rem(zl + j, 2)
            block_send(which, source, target, recv, to_y * 2 + to_z).start()
            return carry

        lax.fori_loop(1, HEADS, send_step, 0)

    def forwards(kind, buf, edge, near, step):
        at_edge = step < 2
        t = 1 - core if at_edge else core
        part = pl.ds(step % 2 * HALF, HALF)
        source = buf.at[1, core + t, part]
        copies = []

        def add(cond, target, recv, f, c, i):
            copies.append((cond, pltpu.make_async_remote_copy(
                src_ref=source, dst_ref=target,
                send_sem=fwd_send.at[kind, step, i], recv_sem=recv,
                device_id=device(f, c, zl, y), device_id_type=MESH,
            )))

        add(has_high, buf.at[0, core + t, part], near.at[0], frame + 1, core, 0)
        add(has_low, buf.at[2, core + t, part], near.at[1], frame - 1, core, 1)
        if at_edge:
            slot = 2 * core
            add(None, buf.at[1, slot, part], edge, frame, 1 - core, 2)
            add(has_high, buf.at[0, slot, part], near.at[0], frame + 1, 1 - core, 3)
            add(has_low, buf.at[2, slot, part], near.at[1], frame - 1, 1 - core, 4)
        return copies

    def each(copies, act):
        for cond, copy in copies:
            if cond is None:
                act(copy)
            else:
                @pl.when(cond)
                def _(copy=copy):
                    act(copy)

    def landed(ref, sem):
        pltpu.make_async_copy(ref, ref, sem).wait()

    def pass_on(kind, buf, recv, edge, near):
        for step in range(4):
            t = 1 - core if step < 2 else core
            part = pl.ds(step % 2 * HALF, HALF)
            landed(buf.at[1, core + t, part], recv.at[t * 2 + step % 2])
            each(forwards(kind, buf, edge, near, step), lambda copy: copy.start())

    def score(which, p):
        count = 2 + which
        t, scores = ((core, s_narrow), (1 - core, s_wide))[which]
        first = core if which == 0 else 0
        q = qb[t]
        k = kb[p, pl.ds(first, count)].reshape(count * TILE, DIM)
        s = lax.dot_general(q, k, (((1,), (1,)), ((), ())), preferred_element_type=jnp.float32)
        scores[p] = s
        best = s[:, :DIM] if p == 1 else m_ref[which]
        for c in range(1 if p == 1 else 0, count * TILE // DIM):
            best = jnp.maximum(best, s[:, c * DIM : (c + 1) * DIM])
        m_ref[which] = best

    def weigh(which, p):
        count = 2 + which
        scores = (s_narrow, s_wide)[which]
        first = core if which == 0 else 0
        s = scores[p]
        best = m_ref[which][:, :1]
        w = jnp.exp2((s - best) * EXP2_SCALE)
        total = w[:, :DIM]
        for c in range(1, count * TILE // DIM):
            total = total + w[:, c * DIM : (c + 1) * DIM]
        v = vb[p, pl.ds(first, count)].reshape(count * TILE, DIM)
        part = lax.dot_general(
            w.astype(jnp.bfloat16), v, (((1,), (0,)), ((), ())), preferred_element_type=jnp.float32
        )
        if p == 1:
            l_ref[which] = total
            acc_ref[which] = part
        else:
            l_ref[which] += total
            acc_ref[which] += part

    def sides(act):
        @pl.when(has_low)
        def _():
            act(0, 0)

        @pl.when(has_high)
        def _():
            act(2, 1)

    pass_on(0, kb, k_recv, k_edge, k_near)
    landed(qb.at[0], q_recv.at[0])
    landed(qb.at[1], q_recv.at[1])
    score(0, 1)
    pass_on(1, vb, v_recv, v_edge, v_near)
    landed(kb.at[1, 2 - 2 * core], k_edge)
    score(1, 1)

    def score_side(p, i):
        landed(kb.at[p], k_near.at[i])
        score(0, p)
        score(1, p)

    sides(score_side)
    for which in range(2):
        m_ref[which] = jnp.broadcast_to(
            jnp.max(m_ref[which], axis=1, keepdims=True), (TILE, DIM)
        )
    weigh(0, 1)
    landed(vb.at[1, 2 - 2 * core], v_edge)
    weigh(1, 1)

    def weigh_side(p, i):
        landed(vb.at[p], v_near.at[i])
        weigh(0, p)

    sides(weigh_side)

    def out_copy(which, i):
        t = (core, 1 - core)[which]
        w, z, c = core * 4 + t * 2 + i // 4, lax.rem(i // 2, 2), lax.rem(i, 2)
        part = osend.at[which, pl.ds(i * TOKENS, TOKENS)]
        here = jnp.logical_and(w * 2 + z == chip, c == core)
        return here, pltpu.make_async_copy(part, ob.at[chip], out_recv), pltpu.make_async_remote_copy(
            src_ref=part, dst_ref=ob.at[chip], send_sem=out_send.at[which, i], recv_sem=out_recv,
            device_id=device(frame, c, z, w), device_id_type=MESH,
        )

    def finish(which):
        total = jnp.sum(l_ref[which], axis=1, keepdims=True)
        osend[which] = (acc_ref[which] / total).astype(jnp.bfloat16)

        def step(i, carry):
            here, local, remote = out_copy(which, i)

            @pl.when(here)
            def _():
                local.start()

            @pl.when(jnp.logical_not(here))
            def _():
                remote.start()

            return carry

        lax.fori_loop(0, SOURCES, step, 0)

    finish(0)
    sides(lambda p, i: weigh(1, p))
    finish(1)

    landed(ob, out_recv)
    for n in range(HEADS):
        o = ob[n].astype(jnp.float32).reshape(3, 4, 4, DIM)
        o_ref[:, :, :, n * DIM : (n + 1) * DIM] = o.astype(jnp.bfloat16)

    for which, source, target, recv in blocks:
        many = source.at[pl.ds(0, HEADS - 1)]
        pltpu.make_async_copy(many, many, own_send.at[which]).wait()
        _, there = block_self(which, source, target, recv)

        @pl.when(jnp.logical_not(own))
        def _(there=there):
            there.wait_send()

    for step in range(4):
        each(forwards(0, kb, k_edge, k_near, step), lambda copy: copy.wait_send())
        each(forwards(1, vb, v_edge, v_near, step), lambda copy: copy.wait_send())

    def out_done(i, carry):
        for which in range(2):
            here, _, remote = out_copy(which, i)

            @pl.when(jnp.logical_not(here))
            def _(remote=remote):
                remote.wait_send()

        return carry

    lax.fori_loop(0, SOURCES, out_done, 0)


def per_device(queries, keys, values, query_gain, key_gain):
    bf16, f32 = jnp.bfloat16, jnp.float32
    dma, vmem = pltpu.SemaphoreType.DMA, pltpu.VMEM
    return pl.pallas_call(
        kernel,
        out_shape=jax.ShapeDtypeStruct(queries.shape, bf16),
        in_specs=[pl.BlockSpec(memory_space=pltpu.VMEM)] * 5,
        out_specs=pl.BlockSpec(memory_space=pltpu.VMEM),
        scratch_shapes=[
            vmem((HEADS, TOKENS, DIM), bf16),
            vmem((HEADS, TOKENS, DIM), bf16),
            vmem((HEADS, TOKENS, DIM), bf16),
            vmem((2, TILE, DIM), bf16),
            vmem((3, 3, TILE, DIM), bf16),
            vmem((3, 3, TILE, DIM), bf16),
            vmem((2, TILE, DIM), bf16),
            vmem((HEADS, TOKENS, DIM), bf16),
            vmem((3, TILE, 2 * TILE), f32),
            vmem((3, TILE, 3 * TILE), f32),
            vmem((2, TILE, DIM), f32),
            vmem((2, TILE, DIM), f32),
            vmem((2, TILE, DIM), f32),
            dma((3,)), dma((3,)), dma((2,)), dma((4,)), dma((4,)), dma, dma, dma((2,)), dma((2,)),
            dma((2, 4, 5)), dma((2, SOURCES)), dma,
        ],
        compiler_params=pltpu.CompilerParams(
            collective_id=0, has_side_effects=True, vmem_limit_bytes=48 * 1024 * 1024
        ),
        cost_estimate=pl.CostEstimate(
            flops=1100000000, bytes_accessed=800000, transcendentals=2200000
        ),
    )(queries, keys, values, query_gain.reshape(1, DIM), key_gain.reshape(1, DIM))


def solution(mesh):
    return jax.shard_map(
        per_device,
        mesh=mesh,
        in_specs=(
            P("ta", "ha", "wa", None),
            P("ta", "ha", "wa", None),
            P("ta", "ha", "wa", None),
            P(),
            P(),
        ),
        out_specs=P("ta", "ha", "wa", None),
        check_vma=False,
    )
```

time: 299 us -> 60.5 us (0.20)
  the two profiles are of different devices: /device:TPU:71 before, /device:TPU:159 now
where the time goes in v1:
time: 60.5 us; the launch traced here: 60.3 us
  Pallas kernels  56.1 us (93%)
  local copies, waits for them, and re-layouts  4.13 us (7%)
    pallas_call x1, Pallas kernels, per_device(): pl.pallas_call(kernel, out_shape=jax.ShapeDtypeStruct(queries.shape, bf16...  56.1 us
    unnamed x11, local copies, waits for them, and re-layouts  4.13 us

profile of v1, /device:TPU:159, one launch (start us, length us, event | category | flops | bytes accessed | tf_op | source)
XLA Modules:
  0.0 60.3 jit_solution(11061282502356583905)
XLA Ops:
  0.0 0.0 copy-start.3
  0.0 0.0 copy-start.4
  0.0 0.7 %copy-done.3 = f32[128]{0:T(128)S(1)} copy-done((f32[128]{0:T(128)S(1)}, f32[128]{0:T(128)}, u32[]{:S(2)}) %copy-start.3) | copy-done | bytes 536
  0.7 0.0 copy-done.4
  0.7 0.0 copy-start
  0.7 0.9 %copy-done = bf16[3,4,4,2048]{3,2,1,0:T(4,128)(2,1)S(1)} copy-done((bf16[3,4,4,2048]{3,2,1,0:T(4,128)(2,1)S(1)}, bf16[3,4,4,2048]{3,2,1,0:T(4,128)(2,1)}, u32[]{:S(2)}) %copy-start) | copy-done | bytes 196632
  1.6 0.0 copy-start.1
  1.6 0.9 %copy-done.1 = bf16[3,4,4,2048]{3,2,1,0:T(4,128)(2,1)S(1)} copy-done((bf16[3,4,4,2048]{3,2,1,0:T(4,128)(2,1)S(1)}, bf16[3,4,4,2048]{3,2,1,0:T(4,128)(2,1)}, u32[]{:S(2)}) %copy-start.1) | copy-done | bytes 196632
  2.5 0.0 copy-start.2
  2.5 0.9 %copy-done.2 = bf16[3,4,4,2048]{3,2,1,0:T(4,128)(2,1)S(1)} copy-done((bf16[3,4,4,2048]{3,2,1,0:T(4,128)(2,1)S(1)}, bf16[3,4,4,2048]{3,2,1,0:T(4,128)(2,1)}, u32[]{:S(2)}) %copy-start.2) | copy-done | bytes 196632
  3.5 56.1 %shard_map.55 = bf16[3,4,4,2048]{3,2,1,0:T(4,128)(2,1)S(1)} custom-call(bf16[3,4,4,2048]{3,2,1,0:T(4,128)(2,1)S(1)} %copy-done, bf16[3,4,4,2048]{3,2,1,0:T(4,128)(2,1)S(1)} %copy-done.1, bf16[3,4,4,2048]{3,2,1,0:T(4,128)(2,1)S(1)} %copy-done.2, f32[1,128]{1,0:T(1,128)S(1)} %bitcast.2, f32[1,128]{1,0:T(1,128)S(1)} %bitcast.3), custom_call_target="tpu_custom_call" | custom-call | flops 1100000000 | bytes 800000 | tf_op jit(solution)/shard_map/pallas_call | solution.py:326
  59.6 0.7 %copy.7 = bf16[3,4,4,2048]{3,2,1,0:T(4,128)(2,1)} copy(bf16[3,4,4,2048]{3,2,1,0:T(4,128)(2,1)S(1)} %shard_map.55) | data formatting | bytes 393216
Async XLA Ops:
  0.0 0.7 %copy-start.3 = (f32[128]{0:T(128)S(1)}, f32[128]{0:T(128)}, u32[]{:S(2)}) copy-start(f32[128]{0:T(128)} %param.8) | copy-start | bytes 1540
  0.0 0.7 %copy-start.4 = (f32[128]{0:T(128)S(1)}, f32[128]{0:T(128)}, u32[]{:S(2)}) copy-start(f32[128]{0:T(128)} %param.9) | copy-start | bytes 1540
  0.7 0.9 %copy-start = (bf16[3,4,4,2048]{3,2,1,0:T(4,128)(2,1)S(1)}, bf16[3,4,4,2048]{3,2,1,0:T(4,128)(2,1)}, u32[]{:S(2)}) copy-start(bf16[3,4,4,2048]{3,2,1,0:T(4,128)(2,1)} %q_ref.1) | copy-start | bytes 589828
  1.6 0.9 %copy-start.1 = (bf16[3,4,4,2048]{3,2,1,0:T(4,128)(2,1)S(1)}, bf16[3,4,4,2048]{3,2,1,0:T(4,128)(2,1)}, u32[]{:S(2)}) copy-start(bf16[3,4,4,2048]{3,2,1,0:T(4,128)(2,1)} %k_ref.1) | copy-start | bytes 589828
  2.5 0.9 %copy-start.2 = (bf16[3,4,4,2048]{3,2,1,0:T(4,128)(2,1)S(1)}, bf16[3,4,4,2048]{3,2,1,0:T(4,128)(2,1)}, u32[]{:S(2)}) copy-start(bf16[3,4,4,2048]{3,2,1,0:T(4,128)(2,1)} %v_ref.1) | copy-start | bytes 589828

commit v2 on v1

v2 whole, which is shorter than its diff:
```python
import math

import jax
import jax.numpy as jnp
from jax import lax
from jax.experimental import pallas as pl
from jax.experimental.pallas import tpu as pltpu
from jax.sharding import PartitionSpec as P

MESH = pl.DeviceIdType.MESH
EPSILON = 1e-06
HEADS = 16
DIM = 128
TOKENS = 48
SOURCES = 8
TILE = SOURCES * TOKENS
HALF = TILE // 2
LINE = 4
SCORE_SCALE = 1.0 / math.sqrt(DIM)

ROUTE = ((3, 3, 0, 0), (1, 2, 3, 0))

ARRIVALS = ((0, 1, 2, 3), (1, 0, 2, 3), (2, 1, 3, 0), (3, 2, 1, 0), (3, 2, 1, 0), (3, 2, 0, 1), (0, 3, 1, 2), (0, 1, 2, 3))
PACKED = tuple(sum(order[turn] * 4**place for place, order in enumerate(ARRIVALS)) for turn in range(4))
POWERS = tuple(4**place for place in range(8))


def normed(x, gain):
    mean_sq = jnp.mean(x * x, axis=-1, keepdims=True)
    return x * lax.rsqrt(mean_sq + EPSILON) * gain


def landed(ref, sem):
    pltpu.make_async_copy(ref, ref, sem).wait()


def kernel(
    q_hbm, k_hbm, v_hbm, qg_ref, kg_ref, o_ref,
    q_in, k_in, v_in, qs, ks, vs, qb, kb, vb, rb, osend, ob,
    s_narrow, s_wide, m_ref, l_ref, acc_ref,
    in_sem, own_send, own_self, q_recv, own_recv, edge_recv, near_recv, cross_recv, relay_recv,
    fwd_send, relay_send, cross_send, out_send, out_recv,
):
    ta, zl, y = lax.axis_index("ta"), lax.axis_index("ha"), lax.axis_index("wa")
    frame, core = ta // 2, lax.rem(ta, 2)
    other = 1 - core
    x = lax.rem(frame, LINE)
    last_frame = lax.axis_size("ta") // 2 - 1
    chip = y * 2 + zl
    to_core = y // 4
    own = core == to_core
    not_own = jnp.logical_not(own)
    has_low, has_high = frame > 0, frame < last_frame
    has = (has_low, has_high)
    first = frame - x
    turn_low = jnp.logical_and(x == 0, has_low)
    turn_high = jnp.logical_and(x == LINE - 1, has_high)
    relay_up = jnp.logical_and(x < LINE - 1, first + LINE <= last_frame)
    relay_down = jnp.logical_and(x > 0, first > 0)

    def device(f, c, z, w):
        return {"ta": f * 2 + c, "ha": z, "wa": w}

    copies_in = [
        pltpu.make_async_copy(src, dst, in_sem.at[i])
        for i, (src, dst) in enumerate(((k_hbm, k_in), (q_hbm, q_in), (v_hbm, v_in)))
    ]
    for copy in copies_in:
        copy.start()

    barrier = pltpu.get_barrier_semaphore()

    def greet(f, c, z, w):
        pl.semaphore_signal(barrier, inc=1, device_id=device(f, c, z, w), device_id_type=MESH)

    def greet_step(n, carry):
        z, c, w = lax.rem(n // 2, 2), lax.rem(n, 2), core * 4 + n // 4

        @pl.when(jnp.logical_or(w * 2 + z != chip, c != core))
        def _():
            greet(frame, c, z, w)

        return carry

    lax.fori_loop(0, HEADS, greet_step, 0)
    greet(frame, other, zl, y)
    for cond, f in (
        (has_low, frame - 1),
        (has_high, frame + 1),
        *((turn_low, frame - LINE + i) for i in range(LINE - 1)),
        *((turn_high, frame + LINE - i) for i in range(LINE - 1)),
        (relay_up, first + LINE - 1),
        (relay_down, first),
    ):
        @pl.when(cond)
        def _(f=f):
            greet(f, core, zl, y)

    def count(cond, amount=1):
        return jnp.where(cond, amount, 0)

    greetings = (
        1 + HEADS - count(own) + count(has_low) + count(has_high)
        + count(turn_low, LINE - 1) + count(turn_high, LINE - 1) + count(relay_up) + count(relay_down)
    )

    col = y // 2
    tile = lax.rem(col, 2)
    rows = pl.ds((lax.rem(y, 2) * 4 + zl * 2 + core) * TOKENS, TOKENS)
    group = lax.rem(y, 4)
    blocks = (
        (0, ks, kb.at[1, col - to_core, rows], own_recv.at[0, group]),
        (1, vs, vb.at[1, col - to_core, rows], own_recv.at[1, group]),
        (2, qs, qb.at[tile, rows], q_recv.at[tile]),
    )

    def block_self(which, source, target, recv):
        return (
            pltpu.make_async_copy(source.at[chip], target, recv),
            pltpu.make_async_remote_copy(
                src_ref=source.at[chip], dst_ref=target,
                send_sem=own_self.at[which], recv_sem=recv,
                device_id=device(frame, other, zl, y), device_id_type=MESH,
            ),
        )

    def send_blocks(which, source, target, recv):
        here, there = block_self(which, source, target, recv)

        @pl.when(own)
        def _():
            here.start()

        @pl.when(not_own)
        def _():
            there.start()

        def send_step(j, carry):
            turn = j // 2
            offset = (turn + 1) // 2 * (2 * lax.rem(turn, 2) - 1)
            to_y = lax.rem(y + offset + 8, 8)
            to_z = lax.rem(zl + j, 2)
            pltpu.make_async_remote_copy(
                src_ref=source.at[to_y * 2 + to_z], dst_ref=target,
                send_sem=own_send.at[which], recv_sem=recv,
                device_id=device(frame, to_core, to_z, to_y), device_id_type=MESH,
            ).start()
            return carry

        lax.fori_loop(1, HEADS, send_step, 0)

    def head(ref, n):
        return ref[:, :, :, n * DIM : (n + 1) * DIM].astype(jnp.float32).reshape(TOKENS, DIM)

    with jax.named_scope("norm_k"):
        copies_in[0].wait()
        for n in range(HEADS):
            ks[n] = normed(head(k_in, n), kg_ref[...]).astype(jnp.bfloat16)
    with jax.named_scope("barrier"):
        pl.semaphore_wait(barrier, greetings)
    with jax.named_scope("sends"):
        send_blocks(*blocks[0])
        copies_in[2].wait()
        for n in range(HEADS):
            vs[n] = head(v_in, n).astype(jnp.bfloat16)
        send_blocks(*blocks[1])
        copies_in[1].wait()
        for n in range(HEADS):
            qs[n] = normed(head(q_in, n), qg_ref[...]).astype(jnp.bfloat16)
        send_blocks(*blocks[2])

    place = lax.rem(y - 4 * core + 8, 8)
    power = jnp.int32(POWERS[0])
    for i in range(1, 8):
        power = jnp.where(place == i, POWERS[i], power)
    bufs = (kb, vb)

    def arriving(turn):
        g = lax.rem(PACKED[turn] // power, 4)
        return g, core + g // 2, pl.ds(lax.rem(g, 2) * HALF, HALF), g // 2 == other

    def forwards(kind, turn):
        buf = bufs[kind]
        g, slot, part, at_edge = arriving(turn)
        copies = []

        def add(i, cond, target, recv, f, c):
            copies.append((cond, pltpu.make_async_remote_copy(
                src_ref=buf.at[1, slot, part], dst_ref=target,
                send_sem=fwd_send.at[kind, turn, i], recv_sem=recv,
                device_id=device(f, c, zl, y), device_id_type=MESH,
            )))

        high = (1, buf.at[0, slot, part], near_recv.at[kind, 0, g], frame + 1, core)
        low = (0, buf.at[2, slot, part], near_recv.at[kind, 1, g], frame - 1, core)
        away = ROUTE[kind][turn]
        if away > 0:
            add(1, turn_high, rb.at[0, kind, turn], relay_recv.at[0, kind, turn], frame - away, core)
            add(0, turn_low, rb.at[1, kind, turn], relay_recv.at[1, kind, turn], frame + away, core)
            add(high[0], jnp.logical_and(has_high, x != LINE - 1), *high[1:])
            add(low[0], jnp.logical_and(has_low, x != 0), *low[1:])
        else:
            add(high[0], has_high, *high[1:])
            add(low[0], has_low, *low[1:])
        add(2, at_edge, buf.at[1, 2 * core, part], edge_recv.at[kind], frame, other)
        return copies

    def each(copies, act):
        for cond, copy in copies:
            @pl.when(cond)
            def _(copy=copy):
                act(copy)

    def pass_on(kind, turns):
        for turn in turns:
            g, slot, part, _ = arriving(turn)
            landed(bufs[kind].at[1, slot, part], own_recv.at[kind, g])
            each(forwards(kind, turn), lambda copy: copy.start())

    def relay_copy(way, kind, turn):
        g, slot, part, _ = arriving(turn)
        return pltpu.make_async_remote_copy(
            src_ref=rb.at[way, kind, turn], dst_ref=bufs[kind].at[2 * way, slot, part],
            send_sem=relay_send.at[way, kind, turn], recv_sem=near_recv.at[kind, way, g],
            device_id=device(first - 1 if way else first + LINE, core, zl, y), device_id_type=MESH,
        )

    def relays(kind, turns, act):
        for turn in turns:
            away = ROUTE[kind][turn]
            if away > 0:
                for way, cond in (
                    (0, jnp.logical_and(relay_up, x == LINE - 1 - away)),
                    (1, jnp.logical_and(relay_down, x == away)),
                ):
                    @pl.when(cond)
                    def _(way=way):
                        act(way, kind, turn)

    def relay(kind, turns):
        def pass_relay(way, kind, turn):
            landed(rb.at[way, kind, turn], relay_recv.at[way, kind, turn])
            relay_copy(way, kind, turn).start()

        relays(kind, turns, pass_relay)

    first_side = count(x == 0)

    def side(turn):
        i = first_side if turn == 0 else 1 - first_side
        return i, jnp.logical_or(jnp.logical_and(i == 0, has_low), jnp.logical_and(i == 1, has_high))

    def cross_copy(kind, i, turn):
        g, slot, part, at_edge = arriving(turn)
        return at_edge, pltpu.make_async_remote_copy(
            src_ref=bufs[kind].at[2 * i, slot, part], dst_ref=bufs[kind].at[2 * i, 2 * core, part],
            send_sem=cross_send.at[kind, i, g], recv_sem=cross_recv.at[kind, i],
            device_id=device(frame, other, zl, y), device_id_type=MESH,
        )

    def near(kind, i):
        for turn in range(4):
            g, slot, part, _ = arriving(turn)
            landed(bufs[kind].at[2 * i, slot, part], near_recv.at[kind, i, g])
            each([cross_copy(kind, i, turn)], lambda copy: copy.start())

    def crossed(kind, i):
        landed(bufs[kind].at[2 * i, 2 * other], cross_recv.at[kind, i])

    def sides(turn, act):
        i, cond = side(turn)

        @pl.when(cond)
        def _():
            act(i)

    def window(buf, which, p):
        start = core if which == 0 else 0
        return buf[p, pl.ds(start, 2 + which)].reshape((2 + which) * TILE, DIM)

    def score(which, p, fresh=False):
        t, scores = ((core, s_narrow), (other, s_wide))[which]
        s = lax.dot_general(
            qb[t], window(kb, which, p), (((1,), (1,)), ((), ())), preferred_element_type=jnp.float32
        ) * SCORE_SCALE
        scores[p] = s
        best = s[:, :DIM] if fresh else jnp.maximum(m_ref[which], s[:, :DIM])
        for c in range(1, (2 + which) * TILE // DIM):
            best = jnp.maximum(best, s[:, c * DIM : (c + 1) * DIM])
        m_ref[which] = best

    def attend(which, p, fresh=False, rows=slice(0, TILE)):
        scores = (s_narrow, s_wide)[which]
        start = core if which == 0 else 0
        best = m_ref[which, rows]
        total, acc = (None, None) if fresh else (l_ref[which, rows], acc_ref[which, rows])
        for c in range(2 + which):
            parts = []
            for d in range(TILE // DIM):
                lanes = slice(c * TILE + d * DIM, c * TILE + (d + 1) * DIM)
                w = jnp.exp(scores[p, rows, lanes] - best)
                total = w if total is None else total + w
                parts.append(w.astype(jnp.bfloat16))
            part = jnp.dot(
                jnp.concatenate(parts, axis=1), vb[p, start + c], preferred_element_type=jnp.float32
            )
            acc = part if acc is None else acc + part
        l_ref[which, rows] = total
        acc_ref[which, rows] = acc

    def out_copy(which, i):
        t = (core, other)[which]
        w, z, c = core * 4 + t * 2 + i // 4, lax.rem(i // 2, 2), lax.rem(i, 2)
        part = osend.at[which, pl.ds(i * TOKENS, TOKENS)]
        here = jnp.logical_and(w * 2 + z == chip, c == core)
        return here, pltpu.make_async_copy(part, ob.at[chip], out_recv), pltpu.make_async_remote_copy(
            src_ref=part, dst_ref=ob.at[chip], send_sem=out_send.at[which, i], recv_sem=out_recv,
            device_id=device(frame, c, z, w), device_id_type=MESH,
        )

    def finish(which, first_block=0, blocks_done=SOURCES):
        rows = slice(first_block * TOKENS, blocks_done * TOKENS)
        total = jnp.sum(l_ref[which, rows], axis=1, keepdims=True)
        osend[which, rows] = (acc_ref[which, rows] / total).astype(jnp.bfloat16)

        def step(i, carry):
            here, local, remote = out_copy(which, i)

            @pl.when(here)
            def _():
                local.start()

            @pl.when(jnp.logical_not(here))
            def _():
                remote.start()

            return carry

        lax.fori_loop(first_block, blocks_done, step, 0)

    for kind in range(2):
        for turn in range(4):
            with jax.named_scope(f"pass{kind}{turn}"):
                pass_on(kind, [turn])
            if kind == 1:
                with jax.named_scope(f"relay{turn}"):
                    relay(turn // 2, [turn % 2])
    with jax.named_scope("near_a"):
        sides(0, lambda i: near(0, i))
    with jax.named_scope("relay_last"):
        relay(1, [2])
    with jax.named_scope("wait_q"):
        landed(qb.at[0], q_recv.at[0])
        landed(qb.at[1], q_recv.at[1])
        landed(kb.at[1, 2 * other], edge_recv.at[0])
    with jax.named_scope("score"):
        score(0, 1, fresh=True)
        score(1, 1, fresh=True)

    def score_side(i):
        crossed(0, i)
        score(0, 2 * i)
        score(1, 2 * i)

    with jax.named_scope("score_a"):
        sides(0, score_side)
    with jax.named_scope("near_b"):
        sides(1, lambda i: near(0, i))
    with jax.named_scope("score_b"):
        sides(1, score_side)
    with jax.named_scope("attend"):
        landed(vb.at[1, 2 * other], edge_recv.at[1])
        for which in range(2):
            m_ref[which] = jnp.broadcast_to(jnp.max(m_ref[which], axis=1, keepdims=True), (TILE, DIM))
        attend(0, 1, fresh=True)
        attend(1, 1, fresh=True)
    with jax.named_scope("near_va"):
        sides(0, lambda i: near(1, i))

    turned = jnp.logical_or(turn_low, turn_high)
    straight = jnp.logical_not(turned)
    with jax.named_scope("near_vb1"):
        @pl.when(straight)
        def _():
            sides(1, lambda i: near(1, i))

    def attend_side(i):
        crossed(1, i)
        attend(0, 2 * i)

    with jax.named_scope("attend_0a"):
        sides(0, attend_side)

    with jax.named_scope("turned"):
        @pl.when(turned)
        def _():
            sides(0, lambda i: attend(1, 2 * i))
            sides(1, lambda i: near(1, i))

    with jax.named_scope("attend_0b"):
        sides(1, attend_side)
        finish(0)
    with jax.named_scope("attend_1a"):
        @pl.when(straight)
        def _():
            sides(0, lambda i: attend(1, 2 * i))

    with jax.named_scope("attend_1b"):
        for first_block in (0, SOURCES // 2):
            rows = slice(first_block * TOKENS, first_block * TOKENS + HALF)
            sides(1, lambda i: attend(1, 2 * i, rows=rows))
            finish(1, first_block, first_block + SOURCES // 2)

    with jax.named_scope("drain"):
        for which, source, target, recv in blocks:
            many = source.at[pl.ds(0, HEADS - 1)]
            landed(many, own_send.at[which])
            _, there = block_self(which, source, target, recv)

            @pl.when(not_own)
            def _(there=there):
                there.wait_send()

        for kind in range(2):
            for turn in range(4):
                each(forwards(kind, turn), lambda copy: copy.wait_send())
                for i in range(2):
                    at_edge, copy = cross_copy(kind, i, turn)

                    @pl.when(jnp.logical_and(at_edge, has[i]))
                    def _(copy=copy):
                        copy.wait_send()

            relays(kind, range(4), lambda way, kind, turn: relay_copy(way, kind, turn).wait_send())

    with jax.named_scope("wait_out"):
        landed(ob, out_recv)
    with jax.named_scope("write_out"):
        for n in range(HEADS):
            o = ob[n].astype(jnp.float32).reshape(3, 4, 4, DIM)
            o_ref[:, :, :, n * DIM : (n + 1) * DIM] = o.astype(jnp.bfloat16)

    with jax.named_scope("drain_out"):
        def out_done(i, carry):
            for which in range(2):
                here, _, remote = out_copy(which, i)

                @pl.when(jnp.logical_not(here))
                def _(remote=remote):
                    remote.wait_send()

            return carry

        lax.fori_loop(0, SOURCES, out_done, 0)


def per_device(queries, keys, values, query_gain, key_gain):
    bf16, f32 = jnp.bfloat16, jnp.float32
    dma, vmem = pltpu.SemaphoreType.DMA, pltpu.VMEM
    hbm = pl.BlockSpec(memory_space=pl.ANY)
    operands = (queries, keys, values, query_gain.reshape(1, DIM), key_gain.reshape(1, DIM))
    block = (HEADS, TOKENS, DIM)
    return pl.pallas_call(
        kernel,
        out_shape=jax.ShapeDtypeStruct(queries.shape, bf16),
        in_specs=[hbm] * 3 + [pl.BlockSpec(memory_space=pltpu.VMEM)] * 2,
        out_specs=pl.BlockSpec(memory_space=pltpu.VMEM),
        scratch_shapes=[
            vmem(queries.shape, bf16), vmem(queries.shape, bf16), vmem(queries.shape, bf16),
            vmem(block, bf16), vmem(block, bf16), vmem(block, bf16),
            vmem((2, TILE, DIM), bf16),
            vmem((3, 3, TILE, DIM), bf16),
            vmem((3, 3, TILE, DIM), bf16),
            vmem((2, 2, 4, HALF, DIM), bf16),
            vmem((2, TILE, DIM), bf16),
            vmem(block, bf16),
            vmem((3, TILE, 2 * TILE), f32),
            vmem((3, TILE, 3 * TILE), f32),
            vmem((2, TILE, DIM), f32),
            vmem((2, TILE, DIM), f32),
            vmem((2, TILE, DIM), f32),
            dma((3,)), dma((3,)), dma((3,)), dma((2,)), dma((2, 4)), dma((2,)), dma((2, 2, 4)),
            dma((2, 2)), dma((2, 2, 4)), dma((2, 4, 3)), dma((2, 2, 4)), dma((2, 2, 4)),
            dma((2, SOURCES)), dma,
        ],
        compiler_params=pltpu.CompilerParams(
            collective_id=0, has_side_effects=True, vmem_limit_bytes=48 * 1024 * 1024
        ),
        cost_estimate=pl.CostEstimate(
            flops=1100000000, bytes_accessed=800000, transcendentals=2200000
        ),
    )(*(pltpu.with_memory_space_constraint(operand, pltpu.HBM) for operand in operands))


def solution(mesh):
    return jax.shard_map(
        per_device,
        mesh=mesh,
        in_specs=(
            P("ta", "ha", "wa", None),
            P("ta", "ha", "wa", None),
            P("ta", "ha", "wa", None),
            P(),
            P(),
        ),
        out_specs=P("ta", "ha", "wa", None),
        check_vma=False,
    )
```

time: 60.5 us -> 43.4 us (0.72)
  the two profiles are of different devices: /device:TPU:159 before, /device:TPU:23 now
where the time goes in v2:
time: 43.4 us; the launch traced here: 43.2 us
  Pallas kernels  42.5 us (98%)
  local copies, waits for them, and re-layouts  0.68 us (2%)
    pallas_call x1, Pallas kernels, per_device(): pl.pallas_call(kernel, out_shape=jax.ShapeDtypeStruct(queries.shape, bf16...  42.5 us

profile of v2, /device:TPU:23, one launch (start us, length us, event | category | flops | bytes accessed | tf_op | source)
XLA Modules:
  0.0 43.2 jit_solution(10773002430084095456)
XLA Ops:
  0.0 42.5 %shard_map.55 = bf16[3,4,4,2048]{3,2,1,0:T(4,128)(2,1)S(1)} custom-call(bf16[3,4,4,2048]{3,2,1,0:T(4,128)(2,1)} %q_hbm.1, bf16[3,4,4,2048]{3,2,1,0:T(4,128)(2,1)} %k_hbm.1, bf16[3,4,4,2048]{3,2,1,0:T(4,128)(2,1)} %v_hbm.1, f32[1,128]{1,0:T(1,128)} %bitcast.2, f32[1,128]{1,0:T(1,128)} %bitcast.3), custom_call_target="tpu_custom_call" | custom-call | flops 1100000000 | bytes 800000 | tf_op jit(solution)/shard_map/pallas_call | solution.py:463
  42.6 0.7 %copy.7 = bf16[3,4,4,2048]{3,2,1,0:T(4,128)(2,1)} copy(bf16[3,4,4,2048]{3,2,1,0:T(4,128)(2,1)S(1)} %shard_map.55) | data formatting | bytes 393216

commit v3 on v2

--- a/solution.py
+++ b/solution.py
@@ -1,3 +1,4 @@
+import functools
 import math
 
 import jax
@@ -17,8 +18,10 @@
 HALF = TILE // 2
 LINE = 4
 SCORE_SCALE = 1.0 / math.sqrt(DIM)
-
-ROUTE = ((3, 3, 0, 0), (1, 2, 3, 0))
+NOTHING = -1e30
+
+ROUTE = ((3, 3, 0, 0), (3, 3, 0, 0))
+AWAY = tuple(sorted({away for turns in ROUTE for away in turns if away > 0}))
 
 ARRIVALS = ((0, 1, 2, 3), (1, 0, 2, 3), (2, 1, 3, 0), (3, 2, 1, 0), (3, 2, 1, 0), (3, 2, 0, 1), (0, 3, 1, 2), (0, 1, 2, 3))
 PACKED = tuple(sum(order[turn] * 4**place for place, order in enumerate(ARRIVALS)) for turn in range(4))
@@ -35,11 +38,11 @@
 
 
 def kernel(
-    q_hbm, k_hbm, v_hbm, qg_ref, kg_ref, o_ref,
-    q_in, k_in, v_in, qs, ks, vs, qb, kb, vb, rb, osend, ob,
+    q_hbm, k_hbm, v_hbm, qg_hbm, kg_hbm, o_ref,
+    q_in, k_in, v_in, qg_ref, kg_ref, qs, ks, vs, qb, kb, vb, rb, osend, ob,
     s_narrow, s_wide, m_ref, l_ref, acc_ref,
     in_sem, own_send, own_self, q_recv, own_recv, edge_recv, near_recv, cross_recv, relay_recv,
-    fwd_send, relay_send, cross_send, out_send, out_recv,
+    fwd_send, relay_send, cross_send, out_send, out_recv, near_ready, up_ready, down_ready,
 ):
     ta, zl, y = lax.axis_index("ta"), lax.axis_index("ha"), lax.axis_index("wa")
     frame, core = ta // 2, lax.rem(ta, 2)
@@ -55,15 +58,22 @@
     first = frame - x
     turn_low = jnp.logical_and(x == 0, has_low)
     turn_high = jnp.logical_and(x == LINE - 1, has_high)
-    relay_up = jnp.logical_and(x < LINE - 1, first + LINE <= last_frame)
-    relay_down = jnp.logical_and(x > 0, first > 0)
+    relay_up, relay_down = (
+        jnp.logical_and(functools.reduce(jnp.logical_or, [x == at for at in places]), exists)
+        for places, exists in (
+            ([LINE - 1 - away for away in AWAY], first + LINE <= last_frame),
+            (AWAY, first > 0),
+        )
+    )
 
     def device(f, c, z, w):
         return {"ta": f * 2 + c, "ha": z, "wa": w}
 
     copies_in = [
         pltpu.make_async_copy(src, dst, in_sem.at[i])
-        for i, (src, dst) in enumerate(((k_hbm, k_in), (q_hbm, q_in), (v_hbm, v_in)))
+        for i, (src, dst) in enumerate(
+            ((k_hbm, k_in), (kg_hbm, kg_ref), (q_hbm, q_in), (qg_hbm, qg_ref), (v_hbm, v_in))
+        )
     ]
     for copy in copies_in:
         copy.start()
@@ -82,15 +92,15 @@
 
         return carry
 
-    lax.fori_loop(0, HEADS, greet_step, 0)
+    with jax.named_scope("greet"):
+        lax.fori_loop(0, HEADS, greet_step, 0)
     greet(frame, other, zl, y)
     for cond, f in (
-        (has_low, frame - 1),
         (has_high, frame + 1),
-        *((turn_low, frame - LINE + i) for i in range(LINE - 1)),
-        *((turn_high, frame + LINE - i) for i in range(LINE - 1)),
         (relay_up, first + LINE - 1),
-        (relay_down, first),
+        (relay_up, first + LINE),
+        *((turn_low, frame + away) for away in AWAY),
+        *((turn_high, frame + 1 + away) for away in AWAY),
     ):
         @pl.when(cond)
         def _(f=f):
@@ -100,9 +110,25 @@
         return jnp.where(cond, amount, 0)
 
     greetings = (
-        1 + HEADS - count(own) + count(has_low) + count(has_high)
-        + count(turn_low, LINE - 1) + count(turn_high, LINE - 1) + count(relay_up) + count(relay_down)
+        1 + HEADS - count(own) + count(has_low)
+        + count(turn_high, len(AWAY)) + count(turn_low, len(AWAY)) + count(relay_down, 2)
     )
+
+    def answer(cond, sem, f):
+        @pl.when(cond)
+        def _():
+            pl.semaphore_signal(sem, inc=1, device_id=device(f, core, zl, y), device_id_type=MESH)
+
+    def answers():
+        answer(has_low, near_ready, frame - 1)
+        for i, away in enumerate(AWAY):
+            answer(turn_low, up_ready, frame - 1 - away)
+            answer(jnp.logical_and(relay_down, x == away), down_ready.at[i], first)
+
+    def ready(cond, sem):
+        @pl.when(cond)
+        def _():
+            pl.semaphore_wait(sem, 1)
 
     col = y // 2
     tile = lax.rem(col, 2)
@@ -124,16 +150,18 @@
             ),
         )
 
-    def send_blocks(which, source, target, recv):
+    def send_blocks(block, begin=0, end=HEADS):
+        which, source, target, recv = block
         here, there = block_self(which, source, target, recv)
 
-        @pl.when(own)
-        def _():
-            here.start()
-
-        @pl.when(not_own)
-        def _():
-            there.start()
+        if begin == 0:
+            @pl.when(own)
+            def _():
+                here.start()
+
+            @pl.when(not_own)
+            def _():
+                there.start()
 
         def send_step(j, carry):
             turn = j // 2
@@ -147,27 +175,29 @@
             ).start()
             return carry
 
-        lax.fori_loop(1, HEADS, send_step, 0)
+        lax.fori_loop(max(begin, 1), end, send_step, 0)
 
     def head(ref, n):
         return ref[:, :, :, n * DIM : (n + 1) * DIM].astype(jnp.float32).reshape(TOKENS, DIM)
 
-    with jax.named_scope("norm_k"):
+    with jax.named_scope("norm_keys"):
         copies_in[0].wait()
+        copies_in[1].wait()
         for n in range(HEADS):
             ks[n] = normed(head(k_in, n), kg_ref[...]).astype(jnp.bfloat16)
     with jax.named_scope("barrier"):
         pl.semaphore_wait(barrier, greetings)
     with jax.named_scope("sends"):
-        send_blocks(*blocks[0])
-        copies_in[2].wait()
+        send_blocks(blocks[0])
+        answers()
+        copies_in[4].wait()
         for n in range(HEADS):
             vs[n] = head(v_in, n).astype(jnp.bfloat16)
-        send_blocks(*blocks[1])
-        copies_in[1].wait()
+        send_blocks(blocks[1])
+        copies_in[2].wait()
+        copies_in[3].wait()
         for n in range(HEADS):
             qs[n] = normed(head(q_in, n), qg_ref[...]).astype(jnp.bfloat16)
-        send_blocks(*blocks[2])
 
     place = lax.rem(y - 4 * core + 8, 8)
     power = jnp.int32(POWERS[0])
@@ -205,6 +235,11 @@
         add(2, at_edge, buf.at[1, 2 * core, part], edge_recv.at[kind], frame, other)
         return copies
 
+    def answered():
+        ready(has_high, near_ready)
+        for i in range(len(AWAY)):
+            ready(turn_low, down_ready.at[i])
+
     def each(copies, act):
         for cond, copy in copies:
             @pl.when(cond)
@@ -215,7 +250,12 @@
         for turn in turns:
             g, slot, part, _ = arriving(turn)
             landed(bufs[kind].at[1, slot, part], own_recv.at[kind, g])
-            each(forwards(kind, turn), lambda copy: copy.start())
+            copies = forwards(kind, turn)
+            if (kind, turn) == (0, 0):
+                each(copies[-2:], lambda copy: copy.start())
+                answered()
+                copies = copies[:-2]
+            each(copies, lambda copy: copy.start())
 
     def relay_copy(way, kind, turn):
         g, slot, part, _ = arriving(turn)
@@ -289,24 +329,23 @@
             best = jnp.maximum(best, s[:, c * DIM : (c + 1) * DIM])
         m_ref[which] = best
 
-    def attend(which, p, fresh=False, rows=slice(0, TILE)):
+    def attend(which, ps, rows, total=None, acc=None):
         scores = (s_narrow, s_wide)[which]
         start = core if which == 0 else 0
         best = m_ref[which, rows]
-        total, acc = (None, None) if fresh else (l_ref[which, rows], acc_ref[which, rows])
-        for c in range(2 + which):
-            parts = []
-            for d in range(TILE // DIM):
-                lanes = slice(c * TILE + d * DIM, c * TILE + (d + 1) * DIM)
-                w = jnp.exp(scores[p, rows, lanes] - best)
-                total = w if total is None else total + w
-                parts.append(w.astype(jnp.bfloat16))
-            part = jnp.dot(
-                jnp.concatenate(parts, axis=1), vb[p, start + c], preferred_element_type=jnp.float32
-            )
-            acc = part if acc is None else acc + part
-        l_ref[which, rows] = total
-        acc_ref[which, rows] = acc
+        for p in ps:
+            for c in range(2 + which):
+                parts = []
+                for d in range(TILE // DIM):
+                    lanes = slice(c * TILE + d * DIM, c * TILE + (d + 1) * DIM)
+                    w = jnp.exp(scores[p, rows, lanes] - best)
+                    total = w if total is None else total + w
+                    parts.append(w.astype(jnp.bfloat16))
+                part = jnp.dot(
+                    jnp.concatenate(parts, axis=1), vb[p, start + c], preferred_element_type=jnp.float32
+                )
+                acc = part if acc is None else acc + part
+        return total, acc
 
     def out_copy(which, i):
         t = (core, other)[which]
@@ -318,11 +357,10 @@
             device_id=device(frame, c, z, w), device_id_type=MESH,
         )
 
-    def finish(which, first_block=0, blocks_done=SOURCES):
-        rows = slice(first_block * TOKENS, blocks_done * TOKENS)
-        total = jnp.sum(l_ref[which, rows], axis=1, keepdims=True)
-        osend[which, rows] = (acc_ref[which, rows] / total).astype(jnp.bfloat16)
-
+    def finish(which, rows, total, acc):
+        osend[which, rows] = (acc / jnp.sum(total, axis=1, keepdims=True)).astype(jnp.bfloat16)
+
+    def send_out(which, begin, end):
         def step(i, carry):
             here, local, remote = out_copy(which, i)
 
@@ -336,20 +374,43 @@
 
             return carry
 
-        lax.fori_loop(first_block, blocks_done, step, 0)
+        lax.fori_loop(begin, end, step, 0)
+
+    @pl.when(jnp.logical_not(jnp.logical_and(has_low, has_high)))
+    def _():
+        absent = 2 * (1 - first_side)
+        s_narrow[absent] = jnp.full((TILE, 2 * TILE), NOTHING, jnp.float32)
+        s_wide[absent] = jnp.full((TILE, 3 * TILE), NOTHING, jnp.float32)
+        vb[absent] = jnp.zeros((3, TILE, DIM), jnp.bfloat16)
 
     for kind in range(2):
         for turn in range(4):
-            with jax.named_scope(f"pass{kind}{turn}"):
+            with jax.named_scope(f"own_blocks_{kind}_{turn}"):
                 pass_on(kind, [turn])
+                if kind == 0:
+                    send_blocks(blocks[2], turn * 4, turn * 4 + 4)
             if kind == 1:
-                with jax.named_scope(f"relay{turn}"):
-                    relay(turn // 2, [turn % 2])
-    with jax.named_scope("near_a"):
+                with jax.named_scope(f"relay_{turn}"):
+                    if turn == 0:
+                        ready(relay_up, up_ready)
+                    if turn < 2:
+                        relay(0, [turn])
+                    if turn == 3:
+                        relay(1, range(2))
+
+    turned = jnp.logical_or(turn_low, turn_high)
+    straight = jnp.logical_not(turned)
+
+    def near_last(cond, kind):
+        @pl.when(cond)
+        def _():
+            sides(1, lambda i: near(kind, i))
+
+    with jax.named_scope("near_keys_first"):
         sides(0, lambda i: near(0, i))
-    with jax.named_scope("relay_last"):
-        relay(1, [2])
-    with jax.named_scope("wait_q"):
+    with jax.named_scope("near_keys_straight"):
+        near_last(straight, 0)
+    with jax.named_scope("queries"):
         landed(qb.at[0], q_recv.at[0])
         landed(qb.at[1], q_recv.at[1])
         landed(kb.at[1, 2 * other], edge_recv.at[0])
@@ -358,60 +419,64 @@
         score(1, 1, fresh=True)
 
     def score_side(i):
+        score(0, 2 * i)
         crossed(0, i)
-        score(0, 2 * i)
         score(1, 2 * i)
 
-    with jax.named_scope("score_a"):
+    with jax.named_scope("score_first_side"):
         sides(0, score_side)
-    with jax.named_scope("near_b"):
-        sides(1, lambda i: near(0, i))
-    with jax.named_scope("score_b"):
+    with jax.named_scope("near_keys_turned"):
+        @pl.when(turned)
+        def _():
+            sides(1, lambda i: near(0, i))
+    with jax.named_scope("near_values_first"):
+        sides(0, lambda i: near(1, i))
+    with jax.named_scope("near_values_firstlues_straight"):
+        near_last(straight, 1)
+    with jax.named_scope("score_last_side"):
         sides(1, score_side)
-    with jax.named_scope("attend"):
+    with jax.named_scope("max"):
         landed(vb.at[1, 2 * other], edge_recv.at[1])
         for which in range(2):
             m_ref[which] = jnp.broadcast_to(jnp.max(m_ref[which], axis=1, keepdims=True), (TILE, DIM))
-        attend(0, 1, fresh=True)
-        attend(1, 1, fresh=True)
-    with jax.named_scope("near_va"):
-        sides(0, lambda i: near(1, i))
-
-    turned = jnp.logical_or(turn_low, turn_high)
-    straight = jnp.logical_not(turned)
-    with jax.named_scope("near_vb1"):
+
+    halves = (slice(0, HALF), slice(HALF, TILE))
+    last_p = 2 * (1 - first_side)
+
+    with jax.named_scope("attend_straight"):
         @pl.when(straight)
         def _():
-            sides(1, lambda i: near(1, i))
-
-    def attend_side(i):
-        crossed(1, i)
-        attend(0, 2 * i)
-
-    with jax.named_scope("attend_0a"):
-        sides(0, attend_side)
-
-    with jax.named_scope("turned"):
+            for turn in range(2):
+                sides(turn, lambda i: crossed(1, i))
+            ps = (1, 2 * first_side, last_p)
+            for rows in halves:
+                finish(0, rows, *attend(0, ps, rows))
+            send_out(0, 0, SOURCES)
+            for half in range(2):
+                finish(1, halves[half], *attend(1, ps, halves[half]))
+                send_out(1, 4 * half, 4 * half + 4)
+
+    with jax.named_scope("attend_turned"):
         @pl.when(turned)
         def _():
-            sides(0, lambda i: attend(1, 2 * i))
-            sides(1, lambda i: near(1, i))
-
-    with jax.named_scope("attend_0b"):
-        sides(1, attend_side)
-        finish(0)
-    with jax.named_scope("attend_1a"):
-        @pl.when(straight)
-        def _():
-            sides(0, lambda i: attend(1, 2 * i))
-
-    with jax.named_scope("attend_1b"):
-        for first_block in (0, SOURCES // 2):
-            rows = slice(first_block * TOKENS, first_block * TOKENS + HALF)
-            sides(1, lambda i: attend(1, 2 * i, rows=rows))
-            finish(1, first_block, first_block + SOURCES // 2)
-
-    with jax.named_scope("drain"):
+            sides(0, lambda i: crossed(1, i))
+            for which in range(2):
+                for rows in halves:
+                    l_ref[which, rows], acc_ref[which, rows] = attend(which, (1, 2 * first_side), rows)
+            with jax.named_scope("near_values_firstlues_turned"):
+                sides(1, lambda i: near(1, i))
+            def last(which, rows):
+                finish(which, rows, *attend(which, (last_p,), rows, l_ref[which, rows], acc_ref[which, rows]))
+
+            for rows in halves:
+                last(0, rows)
+            send_out(0, 0, SOURCES)
+            sides(1, lambda i: crossed(1, i))
+            for half in range(2):
+                last(1, halves[half])
+                send_out(1, 4 * half, 4 * half + 4)
+
+    with jax.named_scope("sends_left"):
         for which, source, target, recv in blocks:
             many = source.at[pl.ds(0, HEADS - 1)]
             landed(many, own_send.at[which])
@@ -433,40 +498,41 @@
 
             relays(kind, range(4), lambda way, kind, turn: relay_copy(way, kind, turn).wait_send())
 
-    with jax.named_scope("wait_out"):
+    with jax.named_scope("outputs_left"):
+        def out_done(i, carry):
+            for which in range(2):
+                here, _, remote = out_copy(which, i)
+
+                @pl.when(jnp.logical_not(here))
+                def _(remote=remote):
+                    remote.wait_send()
+
+            return carry
+
+        lax.fori_loop(0, SOURCES, out_done, 0)
+
+    with jax.named_scope("outputs_land"):
         landed(ob, out_recv)
     with jax.named_scope("write_out"):
         for n in range(HEADS):
             o = ob[n].astype(jnp.float32).reshape(3, 4, 4, DIM)
             o_ref[:, :, :, n * DIM : (n + 1) * DIM] = o.astype(jnp.bfloat16)
 
-    with jax.named_scope("drain_out"):
-        def out_done(i, carry):
-            for which in range(2):
-                here, _, remote = out_copy(which, i)
-
-                @pl.when(jnp.logical_not(here))
-                def _(remote=remote):
-                    remote.wait_send()
-
-            return carry
-
-        lax.fori_loop(0, SOURCES, out_done, 0)
-
 
 def per_device(queries, keys, values, query_gain, key_gain):
     bf16, f32 = jnp.bfloat16, jnp.float32
-    dma, vmem = pltpu.SemaphoreType.DMA, pltpu.VMEM
+    dma, regular, vmem = pltpu.SemaphoreType.DMA, pltpu.SemaphoreType.REGULAR, pltpu.VMEM
     hbm = pl.BlockSpec(memory_space=pl.ANY)
     operands = (queries, keys, values, query_gain.reshape(1, DIM), key_gain.reshape(1, DIM))
     block = (HEADS, TOKENS, DIM)
     return pl.pallas_call(
         kernel,
         out_shape=jax.ShapeDtypeStruct(queries.shape, bf16),
-        in_specs=[hbm] * 3 + [pl.BlockSpec(memory_space=pltpu.VMEM)] * 2,
+        in_specs=[hbm] * 5,
         out_specs=pl.BlockSpec(memory_space=pltpu.VMEM),
         scratch_shapes=[
             vmem(queries.shape, bf16), vmem(queries.shape, bf16), vmem(queries.shape, bf16),
+            vmem((1, DIM), f32), vmem((1, DIM), f32),
             vmem(block, bf16), vmem(block, bf16), vmem(block, bf16),
             vmem((2, TILE, DIM), bf16),
             vmem((3, 3, TILE, DIM), bf16),
@@ -479,9 +545,9 @@
             vmem((2, TILE, DIM), f32),
             vmem((2, TILE, DIM), f32),
             vmem((2, TILE, DIM), f32),
-            dma((3,)), dma((3,)), dma((3,)), dma((2,)), dma((2, 4)), dma((2,)), dma((2, 2, 4)),
+            dma((5,)), dma((3,)), dma((3,)), dma((2,)), dma((2, 4)), dma((2,)), dma((2, 2, 4)),
             dma((2, 2)), dma((2, 2, 4)), dma((2, 4, 3)), dma((2, 2, 4)), dma((2, 2, 4)),
-            dma((2, SOURCES)), dma,
+            dma((2, SOURCES)), dma, regular, regular, regular((len(AWAY),)),
         ],
         compiler_params=pltpu.CompilerParams(
             collective_id=0, has_side_effects=True, vmem_limit_bytes=48 * 1024 * 1024

time: 43.4 us -> 40.7 us (0.938)
  Pallas kernels: 42.5 us -> 39.9 us
    pallas_call x1, Pallas kernels: 42.5 us -> 39.9 us  [per_device(): pl.pallas_call(kernel, out_shape=jax.ShapeDtypeStruct(queries.shape, bf16...]
where the time goes in v3:
time: 40.7 us; the launch traced here: 40.6 us
  Pallas kernels  39.9 us (98%)
  local copies, waits for them, and re-layouts  0.68 us (2%)
    pallas_call x1, Pallas kernels, per_device(): pl.pallas_call(kernel, out_shape=jax.ShapeDtypeStruct(queries.shape, bf16...  39.9 us

profile of v3, /device:TPU:23, one launch (start us, length us, event | category | flops | bytes accessed | tf_op | source)
XLA Modules:
  0.0 40.6 jit_solution(2837084319528977569)
XLA Ops:
  0.0 39.9 %shard_map.55 = bf16[3,4,4,2048]{3,2,1,0:T(4,128)(2,1)S(1)} custom-call(bf16[3,4,4,2048]{3,2,1,0:T(4,128)(2,1)} %q_hbm.1, bf16[3,4,4,2048]{3,2,1,0:T(4,128)(2,1)} %k_hbm.1, bf16[3,4,4,2048]{3,2,1,0:T(4,128)(2,1)} %v_hbm.1, f32[1,128]{1,0:T(1,128)} %bitcast.2, f32[1,128]{1,0:T(1,128)} %bitcast.3), custom_call_target="tpu_custom_call" | custom-call | flops 1100000000 | bytes 800000 | tf_op jit(solution)/shard_map/pallas_call | solution.py:528
  39.9 0.7 %copy.7 = bf16[3,4,4,2048]{3,2,1,0:T(4,128)(2,1)} copy(bf16[3,4,4,2048]{3,2,1,0:T(4,128)(2,1)S(1)} %shard_map.55) | data formatting | bytes 393216

commit v4 on v3

--- a/solution.py
+++ b/solution.py
@@ -20,8 +20,16 @@
 SCORE_SCALE = 1.0 / math.sqrt(DIM)
 NOTHING = -1e30
 
-ROUTE = ((3, 3, 0, 0), (3, 3, 0, 0))
+ROUTE = ((3, 3, 1, 0), (3, 3, 0, 0))
 AWAY = tuple(sorted({away for turns in ROUTE for away in turns if away > 0}))
+
+RELAYS = {
+    (0, 2): ((1, 0, 0),),
+    (0, 3): ((1, 0, 1),),
+    (1, 1): ((0, 0, 0), (1, 1, 0), (0, 0, 2), (1, 0, 2)),
+    (1, 2): ((0, 0, 1),),
+    (1, 3): ((1, 1, 1), (0, 1, 0), (0, 1, 1)),
+}
 
 ARRIVALS = ((0, 1, 2, 3), (1, 0, 2, 3), (2, 1, 3, 0), (3, 2, 1, 0), (3, 2, 1, 0), (3, 2, 0, 1), (0, 3, 1, 2), (0, 1, 2, 3))
 PACKED = tuple(sum(order[turn] * 4**place for place, order in enumerate(ARRIVALS)) for turn in range(4))
@@ -83,17 +91,18 @@
     def greet(f, c, z, w):
         pl.semaphore_signal(barrier, inc=1, device_id=device(f, c, z, w), device_id_type=MESH)
 
-    def greet_step(n, carry):
-        z, c, w = lax.rem(n // 2, 2), lax.rem(n, 2), core * 4 + n // 4
-
-        @pl.when(jnp.logical_or(w * 2 + z != chip, c != core))
-        def _():
-            greet(frame, c, z, w)
-
-        return carry
-
     with jax.named_scope("greet"):
-        lax.fori_loop(0, HEADS, greet_step, 0)
+        for away in (2, 1, 3, 0):
+            w = core * 4 + lax.rem(y + away, 4)
+            for z in (1 - zl, zl):
+                for c in (other, core):
+                    if away == 0 and z is zl and c is core:
+                        @pl.when(not_own)
+                        def _(w=w, z=z, c=c):
+                            greet(frame, c, z, w)
+                    else:
+                        greet(frame, c, z, w)
+
     greet(frame, other, zl, y)
     for cond, f in (
         (has_high, frame + 1),
@@ -163,19 +172,15 @@
             def _():
                 there.start()
 
-        def send_step(j, carry):
+        for j in range(max(begin, 1), end):
             turn = j // 2
-            offset = (turn + 1) // 2 * (2 * lax.rem(turn, 2) - 1)
-            to_y = lax.rem(y + offset + 8, 8)
-            to_z = lax.rem(zl + j, 2)
+            offset = (turn + 1) // 2 * (2 * (turn % 2) - 1)
+            to_y, to_z = lax.rem(y + offset + 8, 8), 1 - zl if j % 2 else zl
             pltpu.make_async_remote_copy(
                 src_ref=source.at[to_y * 2 + to_z], dst_ref=target,
                 send_sem=own_send.at[which], recv_sem=recv,
                 device_id=device(frame, to_core, to_z, to_y), device_id_type=MESH,
             ).start()
-            return carry
-
-        lax.fori_loop(max(begin, 1), end, send_step, 0)
 
     def head(ref, n):
         return ref[:, :, :, n * DIM : (n + 1) * DIM].astype(jnp.float32).reshape(TOKENS, DIM)
@@ -265,7 +270,7 @@
             device_id=device(first - 1 if way else first + LINE, core, zl, y), device_id_type=MESH,
         )
 
-    def relays(kind, turns, act):
+    def relays(kind, turns, act, ways=(0, 1)):
         for turn in turns:
             away = ROUTE[kind][turn]
             if away > 0:
@@ -273,16 +278,17 @@
                     (0, jnp.logical_and(relay_up, x == LINE - 1 - away)),
                     (1, jnp.logical_and(relay_down, x == away)),
                 ):
-                    @pl.when(cond)
-                    def _(way=way):
-                        act(way, kind, turn)
-
-    def relay(kind, turns):
+                    if way in ways:
+                        @pl.when(cond)
+                        def _(way=way):
+                            act(way, kind, turn)
+
+    def relay(kind, turns, ways):
         def pass_relay(way, kind, turn):
             landed(rb.at[way, kind, turn], relay_recv.at[way, kind, turn])
             relay_copy(way, kind, turn).start()
 
-        relays(kind, turns, pass_relay)
+        relays(kind, turns, pass_relay, ways)
 
     first_side = count(x == 0)
 
@@ -349,7 +355,7 @@
 
     def out_copy(which, i):
         t = (core, other)[which]
-        w, z, c = core * 4 + t * 2 + i // 4, lax.rem(i // 2, 2), lax.rem(i, 2)
+        w, z, c = core * 4 + t * 2 + i // 4, i // 2 % 2, i % 2
         part = osend.at[which, pl.ds(i * TOKENS, TOKENS)]
         here = jnp.logical_and(w * 2 + z == chip, c == core)
         return here, pltpu.make_async_copy(part, ob.at[chip], out_recv), pltpu.make_async_remote_copy(
@@ -361,20 +367,16 @@
         osend[which, rows] = (acc / jnp.sum(total, axis=1, keepdims=True)).astype(jnp.bfloat16)
 
     def send_out(which, begin, end):
-        def step(i, carry):
+        for i in range(begin, end):
             here, local, remote = out_copy(which, i)
 
             @pl.when(here)
-            def _():
+            def _(local=local):
                 local.start()
 
             @pl.when(jnp.logical_not(here))
-            def _():
+            def _(remote=remote):
                 remote.start()
-
-            return carry
-
-        lax.fori_loop(begin, end, step, 0)
 
     @pl.when(jnp.logical_not(jnp.logical_and(has_low, has_high)))
     def _():
@@ -389,14 +391,11 @@
                 pass_on(kind, [turn])
                 if kind == 0:
                     send_blocks(blocks[2], turn * 4, turn * 4 + 4)
-            if kind == 1:
-                with jax.named_scope(f"relay_{turn}"):
-                    if turn == 0:
+            with jax.named_scope(f"relay_{kind}_{turn}"):
+                for way, relay_kind, relay_turn in RELAYS.get((kind, turn), ()):
+                    if (way, relay_kind, relay_turn) == (0, 0, 0):
                         ready(relay_up, up_ready)
-                    if turn < 2:
-                        relay(0, [turn])
-                    if turn == 3:
-                        relay(1, range(2))
+                    relay(relay_kind, [relay_turn], (way,))
 
     turned = jnp.logical_or(turn_low, turn_high)
     straight = jnp.logical_not(turned)
@@ -406,9 +405,9 @@
         def _():
             sides(1, lambda i: near(kind, i))
 
-    with jax.named_scope("near_keys_first"):
+    with jax.named_scope("first_side_keys"):
         sides(0, lambda i: near(0, i))
-    with jax.named_scope("near_keys_straight"):
+    with jax.named_scope("straight_keys"):
         near_last(straight, 0)
     with jax.named_scope("queries"):
         landed(qb.at[0], q_recv.at[0])
@@ -425,13 +424,13 @@
 
     with jax.named_scope("score_first_side"):
         sides(0, score_side)
-    with jax.named_scope("near_keys_turned"):
+    with jax.named_scope("turned_keys"):
         @pl.when(turned)
         def _():
             sides(1, lambda i: near(0, i))
-    with jax.named_scope("near_values_first"):
+    with jax.named_scope("first_side_values"):
         sides(0, lambda i: near(1, i))
-    with jax.named_scope("near_values_firstlues_straight"):
+    with jax.named_scope("straight_values"):
         near_last(straight, 1)
     with jax.named_scope("score_last_side"):
         sides(1, score_side)
@@ -443,38 +442,26 @@
     halves = (slice(0, HALF), slice(HALF, TILE))
     last_p = 2 * (1 - first_side)
 
-    with jax.named_scope("attend_straight"):
-        @pl.when(straight)
-        def _():
-            for turn in range(2):
-                sides(turn, lambda i: crossed(1, i))
-            ps = (1, 2 * first_side, last_p)
-            for rows in halves:
-                finish(0, rows, *attend(0, ps, rows))
-            send_out(0, 0, SOURCES)
-            for half in range(2):
-                finish(1, halves[half], *attend(1, ps, halves[half]))
-                send_out(1, 4 * half, 4 * half + 4)
-
-    with jax.named_scope("attend_turned"):
-        @pl.when(turned)
-        def _():
-            sides(0, lambda i: crossed(1, i))
-            for which in range(2):
-                for rows in halves:
-                    l_ref[which, rows], acc_ref[which, rows] = attend(which, (1, 2 * first_side), rows)
-            with jax.named_scope("near_values_firstlues_turned"):
-                sides(1, lambda i: near(1, i))
-            def last(which, rows):
-                finish(which, rows, *attend(which, (last_p,), rows, l_ref[which, rows], acc_ref[which, rows]))
-
-            for rows in halves:
-                last(0, rows)
-            send_out(0, 0, SOURCES)
-            sides(1, lambda i: crossed(1, i))
-            for half in range(2):
-                last(1, halves[half])
-                send_out(1, 4 * half, 4 * half + 4)
+    def gather(which, rows):
+        l_ref[which, rows], acc_ref[which, rows] = attend(which, (1, 2 * first_side), rows)
+
+    def last(which, rows):
+        finish(which, rows, *attend(which, (last_p,), rows, l_ref[which, rows], acc_ref[which, rows]))
+
+    with jax.named_scope("attend_first"):
+        gather(0, slice(0, TILE))
+        sides(0, lambda i: crossed(1, i))
+        gather(1, slice(0, TILE))
+    with jax.named_scope("turned_values"):
+        near_last(turned, 1)
+    with jax.named_scope("attend_last"):
+        for rows in halves:
+            last(0, rows)
+        send_out(0, 0, SOURCES)
+        sides(1, lambda i: crossed(1, i))
+        for half in range(2):
+            last(1, halves[half])
+            send_out(1, 4 * half, 4 * half + 4)
 
     with jax.named_scope("sends_left"):
         for which, source, target, recv in blocks:
@@ -499,17 +486,13 @@
             relays(kind, range(4), lambda way, kind, turn: relay_copy(way, kind, turn).wait_send())
 
     with jax.named_scope("outputs_left"):
-        def out_done(i, carry):
+        for i in range(SOURCES):
             for which in range(2):
                 here, _, remote = out_copy(which, i)
 
                 @pl.when(jnp.logical_not(here))
                 def _(remote=remote):
                     remote.wait_send()
-
-            return carry
-
-        lax.fori_loop(0, SOURCES, out_done, 0)
 
     with jax.named_scope("outputs_land"):
         landed(ob, out_recv)

time: 40.7 us -> 40.1 us (0.985)
  Pallas kernels: 39.9 us -> 39.3 us
    pallas_call x1, Pallas kernels: 39.9 us -> 39.3 us  [per_device(): pl.pallas_call(kernel, out_shape=jax.ShapeDtypeStruct(queries.shape, bf16...]
where the time goes in v4:
time: 40.1 us; the launch traced here: 40 us
  Pallas kernels  39.3 us (98%)
  local copies, waits for them, and re-layouts  0.68 us (2%)
    pallas_call x1, Pallas kernels, per_device(): pl.pallas_call(kernel, out_shape=jax.ShapeDtypeStruct(queries.shape, bf16...  39.3 us

profile of v4, /device:TPU:23, one launch (start us, length us, event | category | flops | bytes accessed | tf_op | source)
XLA Modules:
  0.0 40.0 jit_solution(17048591595319816709)
XLA Ops:
  0.0 39.3 %shard_map.55 = bf16[3,4,4,2048]{3,2,1,0:T(4,128)(2,1)S(1)} custom-call(bf16[3,4,4,2048]{3,2,1,0:T(4,128)(2,1)} %q_hbm.1, bf16[3,4,4,2048]{3,2,1,0:T(4,128)(2,1)} %k_hbm.1, bf16[3,4,4,2048]{3,2,1,0:T(4,128)(2,1)} %v_hbm.1, f32[1,128]{1,0:T(1,128)} %bitcast.2, f32[1,128]{1,0:T(1,128)} %bitcast.3), custom_call_target="tpu_custom_call" | custom-call | flops 1100000000 | bytes 800000 | tf_op jit(solution)/shard_map/pallas_call | solution.py:511
  39.3 0.7 %copy.7 = bf16[3,4,4,2048]{3,2,1,0:T(4,128)(2,1)} copy(bf16[3,4,4,2048]{3,2,1,0:T(4,128)(2,1)S(1)} %shard_map.55) | data formatting | bytes 393216

commit v5 on v4

--- a/solution.py
+++ b/solution.py
@@ -64,6 +64,7 @@
     has_low, has_high = frame > 0, frame < last_frame
     has = (has_low, has_high)
     first = frame - x
+    at_end = jnp.logical_or(x == 0, x == LINE - 1)
     turn_low = jnp.logical_and(x == 0, has_low)
     turn_high = jnp.logical_and(x == LINE - 1, has_high)
     relay_up, relay_down = (
@@ -198,7 +199,10 @@
         copies_in[4].wait()
         for n in range(HEADS):
             vs[n] = head(v_in, n).astype(jnp.bfloat16)
-        send_blocks(blocks[1])
+        @pl.when(at_end)
+        def _():
+            send_blocks(blocks[1])
+
         copies_in[2].wait()
         copies_in[3].wait()
         for n in range(HEADS):
@@ -389,6 +393,11 @@
         for turn in range(4):
             with jax.named_scope(f"own_blocks_{kind}_{turn}"):
                 pass_on(kind, [turn])
+                if (kind, turn) == (0, 0):
+                    @pl.when(jnp.logical_not(at_end))
+                    def _():
+                        send_blocks(blocks[1])
+
                 if kind == 0:
                     send_blocks(blocks[2], turn * 4, turn * 4 + 4)
             with jax.named_scope(f"relay_{kind}_{turn}"):

time: 40.1 us -> 40.1 us (level)
  the two profiles are of different devices: /device:TPU:23 before, /device:TPU:135 now
where the time goes in v5:
time: 40.1 us; the launch traced here: 39.9 us
  Pallas kernels  39.3 us (98%)
  local copies, waits for them, and re-layouts  0.68 us (2%)
    pallas_call x1, Pallas kernels, per_device(): pl.pallas_call(kernel, out_shape=jax.ShapeDtypeStruct(queries.shape, bf16...  39.3 us

profile of v5, /device:TPU:135, one launch (start us, length us, event | category | flops | bytes accessed | tf_op | source)
XLA Modules:
  0.0 39.9 jit_solution(9541719146102374823)
XLA Ops:
  0.0 39.3 %shard_map.55 = bf16[3,4,4,2048]{3,2,1,0:T(4,128)(2,1)S(1)} custom-call(bf16[3,4,4,2048]{3,2,1,0:T(4,128)(2,1)} %q_hbm.1, bf16[3,4,4,2048]{3,2,1,0:T(4,128)(2,1)} %k_hbm.1, bf16[3,4,4,2048]{3,2,1,0:T(4,128)(2,1)} %v_hbm.1, f32[1,128]{1,0:T(1,128)} %bitcast.2, f32[1,128]{1,0:T(1,128)} %bitcast.3), custom_call_target="tpu_custom_call" | custom-call | flops 1100000000 | bytes 800000 | tf_op jit(solution)/shard_map/pallas_call | solution.py:520
  39.3 0.7 %copy.7 = bf16[3,4,4,2048]{3,2,1,0:T(4,128)(2,1)} copy(bf16[3,4,4,2048]{3,2,1,0:T(4,128)(2,1)S(1)} %shard_map.55) | data formatting | bytes 393216

commit v6 on v4

--- a/solution.py
+++ b/solution.py
@@ -20,14 +20,14 @@
 SCORE_SCALE = 1.0 / math.sqrt(DIM)
 NOTHING = -1e30
 
-ROUTE = ((3, 3, 1, 0), (3, 3, 0, 0))
+ROUTE = ((1, 3, 3, 0), (3, 3, 0, 0))
 AWAY = tuple(sorted({away for turns in ROUTE for away in turns if away > 0}))
 
 RELAYS = {
-    (0, 2): ((1, 0, 0),),
-    (0, 3): ((1, 0, 1),),
-    (1, 1): ((0, 0, 0), (1, 1, 0), (0, 0, 2), (1, 0, 2)),
-    (1, 2): ((0, 0, 1),),
+    (0, 3): ((1, 0, 1), (0, 0, 0), (1, 0, 0)),
+    (1, 0): ((1, 0, 2),),
+    (1, 1): ((0, 0, 1), (1, 1, 0)),
+    (1, 2): ((0, 0, 2),),
     (1, 3): ((1, 1, 1), (0, 1, 0), (0, 1, 1)),
 }
 

time: 40.1 us -> 40.3 us (level)
  the two profiles are of different devices: /device:TPU:23 before, /device:TPU:151 now
where the time goes in v6:
time: 40.3 us; the launch traced here: 40.2 us
  Pallas kernels  39.5 us (98%)
  local copies, waits for them, and re-layouts  0.68 us (2%)
    pallas_call x1, Pallas kernels, per_device(): pl.pallas_call(kernel, out_shape=jax.ShapeDtypeStruct(queries.shape, bf16...  39.5 us

profile of v6, /device:TPU:151, one launch (start us, length us, event | category | flops | bytes accessed | tf_op | source)
XLA Modules:
  0.0 40.2 jit_solution(8092281873443025168)
XLA Ops:
  0.0 39.5 %shard_map.55 = bf16[3,4,4,2048]{3,2,1,0:T(4,128)(2,1)S(1)} custom-call(bf16[3,4,4,2048]{3,2,1,0:T(4,128)(2,1)} %q_hbm.1, bf16[3,4,4,2048]{3,2,1,0:T(4,128)(2,1)} %k_hbm.1, bf16[3,4,4,2048]{3,2,1,0:T(4,128)(2,1)} %v_hbm.1, f32[1,128]{1,0:T(1,128)} %bitcast.2, f32[1,128]{1,0:T(1,128)} %bitcast.3), custom_call_target="tpu_custom_call" | custom-call | flops 1100000000 | bytes 800000 | tf_op jit(solution)/shard_map/pallas_call | solution.py:511
  39.5 0.7 %copy.7 = bf16[3,4,4,2048]{3,2,1,0:T(4,128)(2,1)} copy(bf16[3,4,4,2048]{3,2,1,0:T(4,128)(2,1)S(1)} %shard_map.55) | data formatting | bytes 393216
